TPU v7x, 32 devices: a whole 2x2x4 slice. The times are simulated.
32 devices in a mesh: groups: 2 (over x), rows: 8 (over z, y), cols: 2 (over core).
Axes of the slice: x: 2, y: 2, z: 4, core: 2. Of those that a mesh axis runs over, the one named last changes fastest.
Arguments:
- embeddings: float32 [8192, 768], P(('groups', 'rows', 'cols')), parts along dimension 0
- cluster_size: int32 [8], P('groups'), parts along dimension 0, may hold values from 192 to 3072, as said below
- cluster_start: int32 [8], P('groups'), parts along dimension 0, may hold values from 0 to 3904, as said below
- live: int32 [8192], P(('groups', 'rows', 'cols')), parts along dimension 0, may hold values 0 or 1
Outputs:
- best: float32 [8192], P(('groups', 'rows', 'cols')), parts along dimension 0
There are 2 independent parts, one for each index of `groups`. A program takes and returns all parts, laid end to end along the dimension named above; each array names one. Nothing has to cross between parts.
Inputs may be any that keep to these rules, and one draw needn't show every extreme that they name: `cluster_size`: clusters are disjoint ranges of rows within the 4096 rows, each of 192 members or more; one of them has exactly 3072 members. Each cluster_start[k] + cluster_size[k] is at most 4096.
All inputs are finite; a program needn't handle non-finite values. No bound on the sum of `live` on one device may be relied on, other than what follows from the above.
Results may differ from a plain program's by a relative error of at most 0.00062.
Values may be sent and summed in bfloat16 or wider, within the bound.
No kernel may reach another device: no remote copies, remote signals or barrier semaphores. Data moves between devices by JAX's collectives and lax.ppermute only.
A program may use at most 64 MiB of HBM per device.

v0:
```python
import jax
import jax.numpy as jnp
from jax import lax
from jax.sharding import PartitionSpec as P


def labels_of(gid, cluster_size, cluster_start):
    inside = (gid[:, None] >= cluster_start[None, :]) & (
        gid[:, None] < cluster_start[None, :] + cluster_size[None, :]
    )
    ids = jnp.arange(cluster_size.shape[0], dtype=jnp.int32)
    return jnp.max(jnp.where(inside, ids[None, :], -1), axis=1)


def tile_max(carry, queries, qlab, qgid, keys, klive, kgid, cluster_size, cluster_start):
    label = labels_of(kgid, cluster_size, cluster_start)
    klab = jnp.where((klive == 1) & (label >= 0), label, -2)

    def compute():
        sim = lax.dot_general(
            queries, keys, (((1,), (1,)), ((), ())), preferred_element_type=jnp.float32
        )
        valid = (qlab[:, None] == klab[None, :]) & (qgid[:, None] != kgid[None, :])
        return jnp.maximum(carry, jnp.max(jnp.where(valid, sim, jnp.float32(-2.0)), axis=1))

    ids = jnp.arange(cluster_size.shape[0], dtype=jnp.int32)
    query_has = jnp.any(qlab[:, None] == ids[None, :], axis=0)
    key_has = jnp.any(klab[:, None] == ids[None, :], axis=0)
    return lax.cond(jnp.any(query_has & key_has), compute, lambda: carry)


def per_device(embeddings, cluster_size, cluster_start, live):
    rows_dev = embeddings.shape[0]
    squares = jnp.sum(embeddings * embeddings, axis=1, keepdims=True)
    normed = (embeddings * lax.rsqrt(squares + 1e-06)).astype(jnp.bfloat16)
    own_gid = lax.axis_index(("rows", "cols")) * rows_dev + jnp.arange(rows_dev, dtype=jnp.int32)
    qlab = labels_of(own_gid, cluster_size, cluster_start)
    init = jnp.full((rows_dev,), -2.0, jnp.float32)
    pieces = (
        lax.all_gather(normed, ("rows", "cols"), axis=0, tiled=True),
        lax.all_gather(live, ("rows", "cols"), axis=0, tiled=True),
    )
    kgid = jnp.arange(pieces[0].shape[0], dtype=jnp.int32)
    peak = tile_max(
        init, normed, qlab, own_gid, pieces[0], pieces[1], kgid, cluster_size, cluster_start
    )
    return jnp.where((live == 1) & (peak > -1.5), peak, jnp.float32(0.0))


def solution(mesh):
    placed = (
        P(("groups", "rows", "cols"), None),
        P("groups"),
        P("groups"),
        P(("groups", "rows", "cols")),
    )
    return jax.shard_map(
        per_device,
        mesh=mesh,
        in_specs=placed,
        out_specs=P(("groups", "rows", "cols")),
        check_vma=False,
    )
```

profile of v0, /device:TPU:0, one launch (start us, length us, event | category | flops | bytes accessed | tf_op | source)
XLA Modules:
  0.0 87.0 jit_solution(4482495070597255926)
XLA Ops:
  6.5 0.0 all-gather.3.cloned.1.call-start
  6.5 1.3 %multiply_reduce_fusion = f32[256]{0:T(256)S(1)} fusion(f32[256,768]{1,0:T(8,128)} %param.6), kind=kLoop, calls=%fused_computation.5 | loop fusion | flops 392960 | bytes 787456 | tf_op jit(solution)/shard_map/reduce_sum | solution.py:34
  7.8 2.0 %multiply_convert_fusion = bf16[256,768]{1,0:T(8,128)(2,1)} fusion(f32[256,768]{1,0:T(8,128)} %param.6, f32[256]{0:T(256)S(1)} %add_rsqrt_fusion), kind=kLoop, calls=%fused_computation.4 | loop fusion | flops 393216 | bytes 1180672 | tf_op jit(solution)/shard_map/convert_element_type | solution.py:35
  9.8 0.0 all-gather.3.cloned.1.call-update
  9.9 23.4 %all-gather = s32[16,1,256]{2,1,0:T(1,128)S(1)} all-gather(s32[1,1,256]{2,1,0:T(1,128)} %bitcast.3), channel_id=1, replica_groups=mesh['groups'=2,'rows'=8,'cols'=2] {'rows','cols'}, dimensions={0}, use_global_device_ids=true | all-gather | bytes 17408 | tf_op jit(solution)/shard_map/all_gather | solution.py:41
  33.3 0.1 compare_reduce_fusion
  33.3 0.7 add.38
  34.0 0.7 select_reduce_fusion.1
  34.8 0.1 fusion.3
  34.9 0.8 select_reduce_fusion
  35.7 0.2 fusion.2
  35.9 0.7 and_reduce_fusion
  37.2 37.4 %all-gather.3.cloned.1.call-done = bf16[4096,768]{1,0:T(8,128)(2,1)} async-done(((bf16[256,768]{1,0:T(8,128)(2,1)}), bf16[4096,768]{1,0:T(8,128)(2,1)}) %all-gather.3.cloned.1.call-update) | async-done | bytes 6291472 | tf_op jit(solution)/shard_map/all_gather | solution.py:40
  74.5 0.0 copy-start
  74.5 5.1 %conditional.1 = (f32[256]{0:T(256)S(1)}) conditional(s32[]{:T(128)} %convert_element_type.6, () %tuple.11, (s32[256]{0:T(256)S(1)}, s32[4096]{0:T(1024)S(1)}, s32[]{:T(128)}, s32[256]{0:T(256)S(1)}, s32[4096]{0:T(1024)S(1)}, /*index=5*/bf16[256,768]{1,0:T(8,128)(2,1)}, bf16[4096,768]{1,0:T(8,128)(2,1)}) %tuple.12), branch_computations={%region_6.7_spmd, %region_7.9_spmd} | conditional | flops 1615855872 | bytes 6724620 | solution.py:29
  74.6 5.0 %fusion = f32[256]{0:T(256)S(1)} fusion(bf16[256,768]{1,0:T(8,128)(2,1)} %get-tuple-element.29, bf16[4096,768]{1,0:T(8,128)(2,1)} %get-tuple-element.30, s32[4096]{0:T(1024)S(1)} %get-tuple-element.28, s32[256]{0:T(256)S(1)} %broadcast_add_fusion, s32[4096]{0:T(1024)S(1)} %get-tuple-element.25, s32[256]{0:T(256)S(1)} %get-tuple-element.24), kind=kOutput, calls=%fused_computation.1 | convolution fusion | flops 1615855360 | bytes 6720512 | tf_op jit(solution)/shard_map/cond/branch_1_fun/dot_general | solution.py:20
  79.6 0.0 copy-done
  79.6 0.6 and_select_fusion.1
  (8 shorter events, 0.0 us)
Async XLA Ops:
  6.5 68.0 %all-gather.3.cloned.1.call-start = ((), (), s32[]{:S(2)}) async-start(), calls=%async_computation | async-start | bytes 6684672 | tf_op jit(solution)/shard_map/all_gather | solution.py:40
  74.5 5.1 %copy-start = (s32[256]{0:T(256)S(1)}, s32[256]{0:T(256)}, u32[]{:S(2)}) copy-start(s32[256]{0:T(256)} %param.9) | copy-start | bytes 3076
Sparse Core Ops, SparseCore 0:
  10.0 64.5 all-gather.2
where the time goes:
time: 87.3 us; the launch traced here: 87 us
  waiting for transfers between devices  37.4 us (43%)
  blocking collectives  23.4 us (27%)
  between operations  14.1 us (16%)
  other arithmetic  7.08 us (8%)
  matrix products  5.05 us (6%)
    all_gather x1, waiting for transfers between devices, per_device(): lax.all_gather(normed, ('rows', 'cols'), axis=0, tiled=True)  37.4 us
    all_gather x1, blocking collectives, per_device(): lax.all_gather(live, ('rows', 'cols'), axis=0, tiled=True)  23.4 us
    dot_general x1, matrix products, compute(): lax.dot_general(queries, keys, (((1,), (1,)), ((), ())), preferred_elemen...  5.05 us
    convert_element_type x1, other arithmetic, per_device(): normed = (embeddings * lax.rsqrt(squares + 1e-06)).astype(jnp.bfloat16)  2.02 us
  transfers between devices with their start and end apart: 1, of which 1 were waited for; matrix products, arithmetic and copies ran while one was open for 4% of the time, Pallas kernels for 0%

commit v1 on v0

v1 whole, which is shorter than its diff:
```python
import functools

import jax
import jax.numpy as jnp
import numpy as np
from jax import lax
from jax.experimental import pallas as pl
from jax.experimental.pallas import tpu as pltpu
from jax.sharding import PartitionSpec as P

AXES = ("rows", "cols")
EMPTY = -2.0

GRID8 = ((2,), (0, 3), (1, 4, 6), (2, 5), (0, 5, 6), (1, 2, 7), (), (3, 4, 6))


def held_sets(chips):
    if chips == 8:
        return GRID8
    cover, seen = [0], {0}
    while len(seen) < chips:
        gain, step = max(
            (len({(s - c) % chips for c in cover} | {(c - s) % chips for c in cover} | seen), -s)
            for s in range(1, chips)
            if s not in cover
        )
        cover.append(-step)
        seen = {(a - b) % chips for a in cover for b in cover}
    return tuple(tuple((c + d) % chips for d in cover[1:]) for c in range(chips))


def steps_of(sets):
    edges = [(s, t) for t, held in enumerate(sets) for s in held]
    n = len(sets)
    degree = max(
        [sum(e[0] == c for e in edges) for c in range(n)] + [sum(e[1] == c for e in edges) for c in range(n)]
    )
    out = [[None] * degree for _ in range(n)]
    inn = [[None] * degree for _ in range(n)]
    color = {}
    for s, t in edges:
        a = out[s].index(None)
        b = inn[t].index(None)
        if a != b:
            path, node, side, want = [], t, 1, a
            while True:
                e = (inn if side else out)[node][want]
                if e is None:
                    break
                path.append(e)
                node = e[0] if side else e[1]
                side, want = 1 - side, a + b - want
            for e in path:
                out[e[0]][color[e]] = inn[e[1]][color[e]] = None
            for e in path:
                color[e] = a + b - color[e]
                out[e[0]][color[e]] = inn[e[1]][color[e]] = e
        color[(s, t)] = a
        out[s][a] = inn[t][a] = (s, t)
    return [[e for e in edges if color[e] == k] for k in range(degree)]


@functools.lru_cache(None)
def plan(chips, rows_dev):
    sets = held_sets(chips)
    steps = steps_of(sets)
    slots = 2 + 2 * len(steps)
    blocks = np.full((2 * chips, slots), -1, np.int32)
    for c in range(chips):
        for core in range(2):
            blocks[2 * c + core, 0] = 2 * c + core
            blocks[2 * c + core, 1] = 2 * c + 1 - core
            for k, step in enumerate(steps):
                for s, t in step:
                    if t == c:
                        blocks[2 * c + core, 2 + 2 * k] = 2 * s + core
                        blocks[2 * c + core, 3 + 2 * k] = 2 * s + 1 - core
    total = 2 * chips
    largest = total * rows_dev * 3 // 4
    work = [[] for _ in range(total)]
    wanted = []
    for a in range(total):
        for b in range(a + 1, total):
            if (b - a - 1) * rows_dev + 1 >= largest:
                continue
            able = [d for d in range(total) if a in blocks[d] and b in blocks[d]]
            assert able, (a, b)
            wanted.append((len(able), a, b, able))
    for _, a, b, able in sorted(wanted):
        d = min(able, key=lambda d: (len(work[d]), d))
        work[d].append((a, b))
    most = max(len(w) for w in work)
    table = np.zeros((total, slots + 1 + 2 * most), np.int32)
    for d in range(total):
        row = list(blocks[d])
        table[d, :slots] = blocks[d]
        table[d, slots] = len(work[d])
        for i, (a, b) in enumerate(work[d]):
            table[d, slots + 1 + 2 * i] = row.index(a)
            table[d, slots + 2 + 2 * i] = row.index(b)
    return steps, table


def labels(gid, size_ref, start_ref):
    label = jnp.full(gid.shape, -1, jnp.int32)
    for k in range(size_ref.shape[0]):
        first = start_ref[k]
        label = jnp.where((gid >= first) & (gid < first + size_ref[k]), k, label)
    return label


def my_block():
    return lax.axis_index("rows") * lax.axis_size("cols") + lax.axis_index("cols")


def norm_kernel(size_ref, start_ref, live_ref, emb_ref, out_ref):
    rows, width = emb_ref.shape
    emb = emb_ref[...]
    squares = jnp.sum(emb * emb, axis=1, keepdims=True)
    normed = emb * lax.rsqrt(squares + 1e-06)
    gid = my_block() * rows + lax.broadcasted_iota(jnp.int32, (1, rows), 1)
    member = labels(gid, size_ref, start_ref) >= 0
    counts = jnp.where(member & (live_ref[...] == 1), jnp.float32(1), jnp.float32(0))
    counts = jnp.broadcast_to(counts, (128, rows)).T[:, :1]
    out_ref[...] = jnp.where(counts > 0, normed, jnp.float32(jnp.nan)).astype(out_ref.dtype)


def pair_kernel(slots, table_ref, size_ref, start_ref, *refs):
    ins, outs = refs[:slots], refs[slots : 2 * slots]
    held, row_label, row_peak, col_peak, sems = refs[2 * slots :]
    rows = held.shape[1]
    me = my_block()
    copies = [pltpu.make_async_copy(ins[k], held.at[k], sems.at[k]) for k in range(slots)]
    for copy in copies:
        copy.start()
    row_peak[...] = jnp.full(row_peak.shape, EMPTY, jnp.float32)
    col_peak[...] = jnp.full(col_peak.shape, EMPTY, jnp.float32)
    for k in range(slots):
        gid = table_ref[me, k] * rows + lax.broadcasted_iota(jnp.int32, (rows, 128), 0)
        row_label[k] = labels(gid, size_ref, start_ref)
    for copy in copies:
        copy.wait()

    def product(a, b, extra=None):
        sim = lax.dot_general(
            held[a], held[b], (((1,), (1,)), ((), ())), preferred_element_type=jnp.float32
        )
        gid = table_ref[me, b] * rows + lax.broadcasted_iota(jnp.int32, (1, rows), 1)
        lab = labels(gid, size_ref, start_ref)
        mine = jnp.concatenate([row_label[a]] * (rows // 128), axis=1)
        valid = (mine == lab) & (sim > -1.5)
        if extra is not None:
            valid = valid & extra
        sim = jnp.where(valid, sim, jnp.float32(EMPTY))
        best = sim[:, :128]
        for c in range(128, rows, 128):
            best = jnp.maximum(best, sim[:, c : c + 128])
        row_peak[a] = jnp.maximum(row_peak[a], best)
        if extra is None:
            col_peak[b] = jnp.maximum(col_peak[b], jnp.max(sim.reshape(rows // 8, 8, rows), axis=0))

    off = lax.broadcasted_iota(jnp.int32, (rows, rows), 0) != lax.broadcasted_iota(
        jnp.int32, (rows, rows), 1
    )
    product(0, 0, off)

    def body(i, carry):
        product(table_ref[me, slots + 1 + 2 * i], table_ref[me, slots + 2 + 2 * i])
        return carry

    lax.fori_loop(0, table_ref[me, slots], body, 0)
    for k in range(slots):
        across = jnp.max(row_peak[k].T, axis=0, keepdims=True)
        outs[k][...] = jnp.maximum(across, jnp.max(col_peak[k], axis=0, keepdims=True))


def last_kernel(steps, table_ref, live_ref, own_ref, sib_ref, *refs):
    backs, out_ref = refs[:-1], refs[-1]
    me = my_block()
    peak = jnp.maximum(own_ref[...], sib_ref[...])
    for k in range(steps):
        peak = jnp.maximum(peak, jnp.where(table_ref[me, k] == 1, backs[k][...], jnp.float32(EMPTY)))
    out_ref[...] = jnp.where((live_ref[...] == 1) & (peak > -1.5), peak, jnp.float32(0.0))


def per_device(chips, embeddings, cluster_size, cluster_start, live):
    rows, width = embeddings.shape
    steps, table = plan(chips, rows)
    slots = 2 + 2 * len(steps)
    smem = pl.BlockSpec(memory_space=pltpu.SMEM)
    vmem = pl.BlockSpec(memory_space=pltpu.VMEM)
    live = live.reshape(1, rows)
    own = pl.pallas_call(
        norm_kernel,
        out_shape=jax.ShapeDtypeStruct((rows, width), jnp.bfloat16),
        in_specs=[smem, smem, vmem, vmem],
        out_specs=vmem,
        compiler_params=pltpu.CompilerParams(vmem_limit_bytes=32 << 20),
    )(cluster_size, cluster_start, live, embeddings)

    swap = [(d, d ^ 1) for d in range(2 * chips)]
    moves = [[(2 * s + c, 2 * t + c) for s, t in step for c in range(2)] for step in steps]
    sibling = lambda x: lax.ppermute(x, AXES, swap)
    held = [own, sibling(own)]
    for move in moves:
        got = lax.ppermute(own, AXES, move)
        held += [got, sibling(got)]

    peaks = pl.pallas_call(
        functools.partial(pair_kernel, slots),
        out_shape=[jax.ShapeDtypeStruct((1, rows), jnp.float32)] * slots,
        in_specs=[smem] * 3 + [pl.BlockSpec(memory_space=pl.ANY)] * slots,
        out_specs=[vmem] * slots,
        scratch_shapes=[
            pltpu.VMEM((slots, rows, width), jnp.bfloat16),
            pltpu.VMEM((slots, rows, 128), jnp.int32),
            pltpu.VMEM((slots, rows, 128), jnp.float32),
            pltpu.VMEM((slots, 8, rows), jnp.float32),
            pltpu.SemaphoreType.DMA((slots,)),
        ],
        compiler_params=pltpu.CompilerParams(vmem_limit_bytes=48 << 20),
    )(jnp.asarray(table), cluster_size, cluster_start, *held)

    across = sibling(jnp.concatenate(peaks[1::2], axis=0))
    backs = []
    for k, move in enumerate(moves):
        both = jnp.maximum(peaks[2 + 2 * k], across[k + 1 : k + 2])
        backs.append(lax.ppermute(both, AXES, [(t, s) for s, t in move]))
    sent = np.zeros((2 * chips, len(steps)), np.int32)
    for k, move in enumerate(moves):
        for s, _ in move:
            sent[s, k] = 1
    best = pl.pallas_call(
        functools.partial(last_kernel, len(steps)),
        out_shape=jax.ShapeDtypeStruct((1, rows), jnp.float32),
        in_specs=[smem] + [vmem] * (3 + len(steps)),
        out_specs=vmem,
    )(jnp.asarray(sent), live, peaks[0], across[:1], *backs)
    return best.reshape(rows)


def solution(mesh):
    placed = (
        P(("groups", "rows", "cols"), None),
        P("groups"),
        P("groups"),
        P(("groups", "rows", "cols")),
    )
    return jax.shard_map(
        functools.partial(per_device, mesh.shape["rows"]),
        mesh=mesh,
        in_specs=placed,
        out_specs=P(("groups", "rows", "cols")),
        check_vma=False,
    )
```

time: 87.3 us -> 53.8 us (0.62)
  starting transfers between devices: 0.01 us -> 26.2 us
  blocking collectives: 23.4 us -> 0 us
  waiting for transfers between devices: 37.4 us -> 16 us
  between operations: 14.1 us -> 0.15 us
  Pallas kernels: 0 us -> 6.91 us
  other arithmetic: 7.08 us -> 0.59 us
  matrix products: 5.05 us -> 0 us
  local copies, waits for them, and re-layouts: 0.02 us -> 3.57 us
    all_gather x1 -> x0, waiting for transfers between devices: 37.4 us -> none  [per_device(): lax.all_gather(normed, ('rows', 'cols'), axis=0, tiled=True)]
    ppermute x0 -> x11, starting transfers between devices: none -> 26.2 us  [the longest x3 15.9 us: per_device(): backs.append(lax.ppermute(both, AXES, [(t, s) for s, t in move]))]
    all_gather x1 -> x0, blocking collectives: 23.4 us -> none  [per_device(): lax.all_gather(live, ('rows', 'cols'), axis=0, tiled=True)]
    ppermute x0 -> x11, waiting for transfers between devices: none -> 16 us  [the longest x3 9.94 us: per_device(): got = lax.ppermute(own, AXES, move)]
    pallas_call x0 -> x3, Pallas kernels: none -> 6.91 us  [the longest x1 4.59 us: per_device(): pl.pallas_call(functools.partial(pair_kernel, slots), out_shape=[jax.Shap...]
    dot_general x1 -> x0, matrix products: 5.05 us -> none  [compute(): lax.dot_general(queries, keys, (((1,), (1,)), ((), ())), preferred_elemen...]
    unnamed x2 -> x20, local copies, waits for them, and re-layouts: 0.01 us -> 3.57 us
    convert_element_type x1 -> x0, other arithmetic: 2.02 us -> none  [per_device(): normed = (embeddings * lax.rsqrt(squares + 1e-06)).astype(jnp.bfloat16)]
  transfers between devices with their start and end apart: 1 -> 11, of which waited for: 1 -> 5; matrix products, arithmetic and copies ran while one was open for 4% -> 0% of each run, Pallas kernels for 0% -> 0%
where the time goes in v1:
time: 53.8 us; the launch traced here: 53.4 us
  starting transfers between devices  26.2 us (49%)
  waiting for transfers between devices  16 us (30%)
  Pallas kernels  6.91 us (13%)
  local copies, waits for them, and re-layouts  3.57 us (7%)
  other arithmetic  0.59 us (1%)
    ppermute x3, starting transfers between devices, per_device(): backs.append(lax.ppermute(both, AXES, [(t, s) for s, t in move]))  15.9 us
    ppermute x3, waiting for transfers between devices, per_device(): got = lax.ppermute(own, AXES, move)  9.94 us
    ppermute x3, starting transfers between devices, per_device(): got = lax.ppermute(own, AXES, move)  9.59 us
    pallas_call x1, Pallas kernels, per_device(): pl.pallas_call(functools.partial(pair_kernel, slots), out_shape=[jax.Shap...  4.59 us
    unnamed x20, local copies, waits for them, and re-layouts  3.57 us
    ppermute x3, waiting for transfers between devices, per_device(): backs.append(lax.ppermute(both, AXES, [(t, s) for s, t in move]))  3.31 us
    ppermute x5, waiting for transfers between devices, per_device(): sibling = lambda x: lax.ppermute(x, AXES, swap)  2.74 us
    pallas_call x1, Pallas kernels, per_device(): pl.pallas_call(functools.partial(last_kernel, len(steps)), out_shape=jax....  1.52 us
  transfers between devices with their start and end apart: 11, of which 5 were waited for; matrix products, arithmetic and copies ran while one was open for 0% of the time, Pallas kernels for 0%

profile of v1, /device:TPU:0, one launch (start us, length us, event | category | flops | bytes accessed | tf_op | source)
XLA Modules:
  0.0 53.4 jit_solution(9820403019572962091)
XLA Ops:
  0.0 0.7 %copy-done.3 = s32[4]{0:T(128)S(1)} copy-done((s32[4]{0:T(128)S(1)}, s32[4]{0:T(128)}, u32[]{:S(2)}) %copy-start.3) | copy-done | bytes 40
  0.7 0.0 copy-done.2
  0.7 1.1 %copy-done = f32[256,768]{1,0:T(8,128)S(1)} copy-done((f32[256,768]{1,0:T(8,128)S(1)}, f32[256,768]{1,0:T(8,128)}, u32[]{:S(2)}) %copy-start) | copy-done | bytes 786456
  1.8 0.7 %copy-done.4 = s32[4]{0:T(128)S(1)} copy-done((s32[4]{0:T(128)S(1)}, s32[4]{0:T(128)}, u32[]{:S(2)}) %copy-start.4) | copy-done | bytes 40
  2.5 0.8 %shard_map.64.refs_0_ = bf16[256,768]{1,0:T(8,128)(2,1)S(1)} custom-call(s32[4]{0:T(128)S(1)} %copy-done.3, s32[4]{0:T(128)S(1)} %copy-done.4, s32[1,256]{1,0:T(1,128)S(1)} %bitcast.3, f32[256,768]{1,0:T(8,128)S(1)} %copy-done), custom_call_target="tpu_custom_call" | custom-call | tf_op jit(solution)/shard_map/pallas_call | solution.py:193
  3.3 0.7 %collective-permute-start.5 = (bf16[256,768]{1,0:T(8,128)(2,1)S(1)}, bf16[256,768]{1,0:T(8,128)(2,1)S(1)}, u32[]{:S(2)}, u32[]{:S(2)}) collective-permute-start(bf16[256,768]{1,0:T(8,128)(2,1)S(1)} %shard_map.64.refs_0_), channel_id=1, source_target_pairs={{8,4},{9,5},{10,8},{11,9},{4,10},{5,11},{12,14},{13,15},{24,20},{2... | collective-permute-start | bytes 1179656 | tf_op jit(solution)/shard_map/ppermute | solution.py:206
  4.0 4.9 %collective-permute-start.3 = (bf16[256,768]{1,0:T(8,128)(2,1)S(1)}, bf16[256,768]{1,0:T(8,128)(2,1)S(1)}, u32[]{:S(2)}, u32[]{:S(2)}) collective-permute-start(bf16[256,768]{1,0:T(8,128)(2,1)S(1)} %shard_map.64.refs_0_), channel_id=1, source_target_pairs={{0,2},{1,3},{2,4},{3,5},{4,6},{5,7},{12,8},{13,9},{14,10},{15,11},... | collective-permute-start | bytes 1179656 | tf_op jit(solution)/shard_map/ppermute | solution.py:206
  8.9 4.0 %collective-permute-start.1 = (bf16[256,768]{1,0:T(8,128)(2,1)S(1)}, bf16[256,768]{1,0:T(8,128)(2,1)S(1)}, u32[]{:S(2)}, u32[]{:S(2)}) collective-permute-start(bf16[256,768]{1,0:T(8,128)(2,1)S(1)} %shard_map.64.refs_0_), channel_id=1, source_target_pairs={{4,0},{5,1},{6,2},{7,3},{12,4},{13,5},{10,6},{11,7},{0,8},{1,9},{2... | collective-permute-start | bytes 1179656 | tf_op jit(solution)/shard_map/ppermute | solution.py:206
  12.9 0.1 collective-permute-start
  13.0 0.0 collective-permute-done.5.refs_6_
  13.0 0.5 collective-permute-start.6
  13.5 3.7 %collective-permute-done.3.refs_4_ = bf16[256,768]{1,0:T(8,128)(2,1)S(1)} collective-permute-done((bf16[256,768]{1,0:T(8,128)(2,1)S(1)}, bf16[256,768]{1,0:T(8,128)(2,1)S(1)}, u32[]{:S(2)}, u32[]{:S(2)}) %collective-permute-start.3) | collective-permute-done | bytes 393248 | tf_op jit(solution)/shard_map/ppermute | solution.py:206
  17.2 0.0 collective-permute-start.4
  17.2 6.2 %collective-permute-done.1.refs_2_ = bf16[256,768]{1,0:T(8,128)(2,1)S(1)} collective-permute-done((bf16[256,768]{1,0:T(8,128)(2,1)S(1)}, bf16[256,768]{1,0:T(8,128)(2,1)S(1)}, u32[]{:S(2)}, u32[]{:S(2)}) %collective-permute-start.1) | collective-permute-done | bytes 393248 | tf_op jit(solution)/shard_map/ppermute | solution.py:206
  23.4 0.0 collective-permute-start.2
  23.4 0.0 collective-permute-done.refs_1_
  23.4 0.0 collective-permute-done.6.refs_7_
  23.5 0.0 collective-permute-done.4.refs_5_
  23.5 1.7 %collective-permute-done.2.refs_3_ = bf16[256,768]{1,0:T(8,128)(2,1)S(1)} collective-permute-done((bf16[256,768]{1,0:T(8,128)(2,1)S(1)}, bf16[256,768]{1,0:T(8,128)(2,1)S(1)}, u32[]{:S(2)}, u32[]{:S(2)}) %collective-permute-start.2) | collective-permute-done | bytes 393248 | tf_op jit(solution)/shard_map/ppermute | solution.py:203
  25.2 4.6 %shard_map.65 = (f32[1,256]{1,0:T(1,128)S(1)}, f32[1,256]{1,0:T(1,128)S(1)}, f32[1,256]{1,0:T(1,128)S(1)}, f32[1,256]{1,0:T(1,128)S(1)}, f32[1,256]{1,0:T(1,128)...) custom-call(s32[16,31]{1,0:T(8,128)S(1)} %copy-done.1, s32[4]{0:T(128)S(1)} %copy-done.3, ...), custom_call_target="tpu_custom_call" | custom-call | tf_op jit(solution)/shard_map/pallas_call | solution.py:209
  29.8 0.5 %copy-done.6 = f32[1,256]{1,0:T(1,128)} copy-done((f32[1,256]{1,0:T(1,128)}, f32[1,256]{1,0:T(1,128)S(1)}, u32[]{:S(2)}) %copy-start.6) | copy-done | bytes 1048
  30.3 0.2 collective-permute-start.7
  30.5 1.0 %collective-permute-done.7 = f32[4,256]{1,0:T(4,128)S(1)} collective-permute-done((f32[4,256]{1,0:T(4,128)S(1)}, f32[4,256]{1,0:T(4,128)S(1)}, u32[]{:S(2)}, u32[]{:S(2)}) %collective-permute-start.7) | collective-permute-done | bytes 4128 | tf_op jit(solution)/shard_map/ppermute | solution.py:203
  31.6 0.6 %slice_maximum_fusion = (f32[1,256]{1,0:T(1,128)S(1)}, f32[1,256]{1,0:T(1,128)S(1)}, f32[1,256]{1,0:T(1,128)S(1)}, f32[1,256]{1,0:T(1,128)}) fusion(f32[1,256]{1,0:T(1,128)S(1)} %get-tuple-element.20, f32[4,256]{1,0:T(4,128)S(1)} %collective-permute-done.7, f32[1,256]{1,0:T(1,128)S(1)} %get-tuple-element.19, f32[1,256]{1,0:T(1,128)S(1)} %get-tuple-element.18), kind=kLoop, calls=%fused_computation.1 | loop fusion | flops 768 | bytes 11264 | tf_op jit(solution)/shard_map/max | solution.py:227
  32.1 0.6 %collective-permute-start.10 = (f32[1,256]{1,0:T(1,128)S(1)}, f32[1,256]{1,0:T(1,128)S(1)}, u32[]{:S(2)}, u32[]{:S(2)}) collective-permute-start(f32[1,256]{1,0:T(1,128)S(1)} %get-tuple-element.21), channel_id=1, source_target_pairs={{4,8},{5,9},{8,10},{9,11},{10,4},{11,5},{14,12},{15,13},{20,24},{2... | collective-permute-start | bytes 3080 | tf_op jit(solution)/shard_map/ppermute | solution.py:228
  32.8 1.3 %collective-permute-start.9 = (f32[1,256]{1,0:T(1,128)S(1)}, f32[1,256]{1,0:T(1,128)S(1)}, u32[]{:S(2)}, u32[]{:S(2)}) collective-permute-start(f32[1,256]{1,0:T(1,128)S(1)} %get-tuple-element.22), channel_id=1, source_target_pairs={{2,0},{3,1},{4,2},{5,3},{6,4},{7,5},{8,12},{9,13},{10,14},{11,15},... | collective-permute-start | bytes 3080 | tf_op jit(solution)/shard_map/ppermute | solution.py:228
  34.1 13.9 %collective-permute-start.8 = (f32[1,256]{1,0:T(1,128)S(1)}, f32[1,256]{1,0:T(1,128)S(1)}, u32[]{:S(2)}, u32[]{:S(2)}) collective-permute-start(f32[1,256]{1,0:T(1,128)S(1)} %get-tuple-element.23), channel_id=1, source_target_pairs={{0,4},{1,5},{2,6},{3,7},{4,12},{5,13},{6,10},{7,11},{8,0},{9,1},{1... | collective-permute-start | bytes 3080 | tf_op jit(solution)/shard_map/ppermute | solution.py:228
  48.0 0.0 collective-permute-done.10.refs_2_
  48.0 0.0 collective-permute-done.9.refs_1_
  48.1 3.3 %collective-permute-done.8.refs_0_ = f32[1,256]{1,0:T(1,128)S(1)} collective-permute-done((f32[1,256]{1,0:T(1,128)S(1)}, f32[1,256]{1,0:T(1,128)S(1)}, u32[]{:S(2)}, u32[]{:S(2)}) %collective-permute-start.8) | collective-permute-done | bytes 1056 | tf_op jit(solution)/shard_map/ppermute | solution.py:228
  51.4 0.5 copy-done.9
  51.9 1.5 %shard_map.66 = f32[1,256]{1,0:T(1,128)} custom-call(s32[16,3]{1,0:T(8,128)} %constant.5.clone.table_ref, s32[1,256]{1,0:T(1,128)} %bitcast.2, f32[1,256]{1,0:T(1,128)} %copy-done.6, f32[1,256]{1,0:T(1,128)} %get-tuple-element.24.sib_ref, f32[1,256]{1,0:T(1,128)} %copy-done.9, f32[1,256]{1,0:T(1,128)} %copy-done.8, f32[1,256]{1,0:T(1,128)} %copy-done.7), custom_call_target="tpu_custom_call" | custom-call | tf_op jit(solution)/shard_map/pallas_call | solution.py:233
  (15 shorter events, 0.0 us)
Async XLA Ops:
  0.0 0.7 %copy-start.3 = (s32[4]{0:T(128)S(1)}, s32[4]{0:T(128)}, u32[]{:S(2)}) copy-start(s32[4]{0:T(128)} %size_ref.3) | copy-start | bytes 52
  0.0 0.7 %copy-start.2 = (s32[256]{0:T(256)S(1)}, s32[256]{0:T(256)}, u32[]{:S(2)}) copy-start(s32[256]{0:T(256)} %param.9) | copy-start | bytes 3076
  0.7 1.1 %copy-start = (f32[256,768]{1,0:T(8,128)S(1)}, f32[256,768]{1,0:T(8,128)}, u32[]{:S(2)}) copy-start(f32[256,768]{1,0:T(8,128)} %emb_ref.1) | copy-start | bytes 2359300
  1.8 0.7 %copy-start.4 = (s32[4]{0:T(128)S(1)}, s32[4]{0:T(128)}, u32[]{:S(2)}) copy-start(s32[4]{0:T(128)} %start_ref.3) | copy-start | bytes 52
  2.5 22.7 %copy-start.1 = (s32[16,31]{1,0:T(8,128)S(1)}, s32[16,31]{1,0:T(8,128)}, u32[]{:S(2)}) copy-start(s32[16,31]{1,0:T(8,128)} %constant.4.clone.table_ref) | copy-start | bytes 5956
  2.5 22.7 %copy-start.5 = (s32[4]{0:T(128)S(1)}, s32[4]{0:T(128)}, u32[]{:S(2)}) copy-start(s32[4]{0:T(128)} %start_ref.3) | copy-start | bytes 52
  3.3 9.7 %collective-permute-start.5 = (bf16[256,768]{1,0:T(8,128)(2,1)S(1)}, bf16[256,768]{1,0:T(8,128)(2,1)S(1)}, u32[]{:S(2)}, u32[]{:S(2)}) collective-permute-start(bf16[256,768]{1,0:T(8,128)(2,1)S(1)} %shard_map.64.refs_0_), channel_id=1, source_target_pairs={{8,4},{9,5},{10,8},{11,9},{4,10},{5,11},{12,14},{13,15},{24,20},{2... | collective-permute-start | bytes 1179656 | tf_op jit(solution)/shard_map/ppermute | solution.py:206
  4.0 13.2 %collective-permute-start.3 = (bf16[256,768]{1,0:T(8,128)(2,1)S(1)}, bf16[256,768]{1,0:T(8,128)(2,1)S(1)}, u32[]{:S(2)}, u32[]{:S(2)}) collective-permute-start(bf16[256,768]{1,0:T(8,128)(2,1)S(1)} %shard_map.64.refs_0_), channel_id=1, source_target_pairs={{0,2},{1,3},{2,4},{3,5},{4,6},{5,7},{12,8},{13,9},{14,10},{15,11},... | collective-permute-start | bytes 1179656 | tf_op jit(solution)/shard_map/ppermute | solution.py:206
  8.9 14.5 %collective-permute-start.1 = (bf16[256,768]{1,0:T(8,128)(2,1)S(1)}, bf16[256,768]{1,0:T(8,128)(2,1)S(1)}, u32[]{:S(2)}, u32[]{:S(2)}) collective-permute-start(bf16[256,768]{1,0:T(8,128)(2,1)S(1)} %shard_map.64.refs_0_), channel_id=1, source_target_pairs={{4,0},{5,1},{6,2},{7,3},{12,4},{13,5},{10,6},{11,7},{0,8},{1,9},{2... | collective-permute-start | bytes 1179656 | tf_op jit(solution)/shard_map/ppermute | solution.py:206
  12.9 10.5 %collective-permute-start = (bf16[256,768]{1,0:T(8,128)(2,1)S(1)}, bf16[256,768]{1,0:T(8,128)(2,1)S(1)}, u32[]{:S(2)}, u32[]{:S(2)}) collective-permute-start(bf16[256,768]{1,0:T(8,128)(2,1)S(1)} %shard_map.64.refs_0_), channel_id=1, source_target_pairs={{0,1},{1,0},{2,3},{3,2},{4,5},{5,4},{6,7},{7,6},{8,9},{9,8},{10,11... | collective-permute-start | bytes 1179656 | tf_op jit(solution)/shard_map/ppermute | solution.py:203
  13.0 10.4 %collective-permute-start.6 = (bf16[256,768]{1,0:T(8,128)(2,1)S(1)}, bf16[256,768]{1,0:T(8,128)(2,1)S(1)}, u32[]{:S(2)}, u32[]{:S(2)}) collective-permute-start(bf16[256,768]{1,0:T(8,128)(2,1)S(1)} %collective-permute-done.5.refs_6_), channel_id=1, source_target_pairs={{0,1},{1,0},{2,3},{3,2},{4,5},{5,4},{6,7},{7,6},{8,9},{9,8},{10,11... | collective-permute-start | bytes 1179656 | tf_op jit(solution)/shard_map/ppermute | solution.py:203
  17.2 6.2 %collective-permute-start.4 = (bf16[256,768]{1,0:T(8,128)(2,1)S(1)}, bf16[256,768]{1,0:T(8,128)(2,1)S(1)}, u32[]{:S(2)}, u32[]{:S(2)}) collective-permute-start(bf16[256,768]{1,0:T(8,128)(2,1)S(1)} %collective-permute-done.3.refs_4_), channel_id=1, source_target_pairs={{0,1},{1,0},{2,3},{3,2},{4,5},{5,4},{6,7},{7,6},{8,9},{9,8},{10,11... | collective-permute-start | bytes 1179656 | tf_op jit(solution)/shard_map/ppermute | solution.py:203
  23.4 1.7 %collective-permute-start.2 = (bf16[256,768]{1,0:T(8,128)(2,1)S(1)}, bf16[256,768]{1,0:T(8,128)(2,1)S(1)}, u32[]{:S(2)}, u32[]{:S(2)}) collective-permute-start(bf16[256,768]{1,0:T(8,128)(2,1)S(1)} %collective-permute-done.1.refs_2_), channel_id=1, source_target_pairs={{0,1},{1,0},{2,3},{3,2},{4,5},{5,4},{6,7},{7,6},{8,9},{9,8},{10,11... | collective-permute-start | bytes 1179656 | tf_op jit(solution)/shard_map/ppermute | solution.py:203
  29.8 0.5 %copy-start.6 = (f32[1,256]{1,0:T(1,128)}, f32[1,256]{1,0:T(1,128)S(1)}, u32[]{:S(2)}) copy-start(f32[1,256]{1,0:T(1,128)S(1)} %get-tuple-element.13.own_ref) | copy-start | bytes 3076
  30.3 1.2 %collective-permute-start.7 = (f32[4,256]{1,0:T(4,128)S(1)}, f32[4,256]{1,0:T(4,128)S(1)}, u32[]{:S(2)}, u32[]{:S(2)}) collective-permute-start(f32[4,256]{1,0:T(4,128)S(1)} %pad_maximum_fusion), channel_id=1, source_target_pairs={{0,1},{1,0},{2,3},{3,2},{4,5},{5,4},{6,7},{7,6},{8,9},{9,8},{10,11... | collective-permute-start | bytes 12296 | tf_op jit(solution)/shard_map/ppermute | solution.py:203
  32.1 15.9 %collective-permute-start.10 = (f32[1,256]{1,0:T(1,128)S(1)}, f32[1,256]{1,0:T(1,128)S(1)}, u32[]{:S(2)}, u32[]{:S(2)}) collective-permute-start(f32[1,256]{1,0:T(1,128)S(1)} %get-tuple-element.21), channel_id=1, source_target_pairs={{4,8},{5,9},{8,10},{9,11},{10,4},{11,5},{14,12},{15,13},{20,24},{2... | collective-permute-start | bytes 3080 | tf_op jit(solution)/shard_map/ppermute | solution.py:228
  32.8 15.2 %collective-permute-start.9 = (f32[1,256]{1,0:T(1,128)S(1)}, f32[1,256]{1,0:T(1,128)S(1)}, u32[]{:S(2)}, u32[]{:S(2)}) collective-permute-start(f32[1,256]{1,0:T(1,128)S(1)} %get-tuple-element.22), channel_id=1, source_target_pairs={{2,0},{3,1},{4,2},{5,3},{6,4},{7,5},{8,12},{9,13},{10,14},{11,15},... | collective-permute-start | bytes 3080 | tf_op jit(solution)/shard_map/ppermute | solution.py:228
  34.1 17.3 %collective-permute-start.8 = (f32[1,256]{1,0:T(1,128)S(1)}, f32[1,256]{1,0:T(1,128)S(1)}, u32[]{:S(2)}, u32[]{:S(2)}) collective-permute-start(f32[1,256]{1,0:T(1,128)S(1)} %get-tuple-element.23), channel_id=1, source_target_pairs={{0,4},{1,5},{2,6},{3,7},{4,12},{5,13},{6,10},{7,11},{8,0},{9,1},{1... | collective-permute-start | bytes 3080 | tf_op jit(solution)/shard_map/ppermute | solution.py:228
  48.0 3.3 %copy-start.7 = (f32[1,256]{1,0:T(1,128)}, f32[1,256]{1,0:T(1,128)S(1)}, u32[]{:S(2)}) copy-start(f32[1,256]{1,0:T(1,128)S(1)} %collective-permute-done.10.refs_2_) | copy-start | bytes 3076
  48.0 3.3 %copy-start.8 = (f32[1,256]{1,0:T(1,128)}, f32[1,256]{1,0:T(1,128)S(1)}, u32[]{:S(2)}) copy-start(f32[1,256]{1,0:T(1,128)S(1)} %collective-permute-done.9.refs_1_) | copy-start | bytes 3076
  51.4 0.5 %copy-start.9 = (f32[1,256]{1,0:T(1,128)}, f32[1,256]{1,0:T(1,128)S(1)}, u32[]{:S(2)}) copy-start(f32[1,256]{1,0:T(1,128)S(1)} %collective-permute-done.8.refs_0_) | copy-start | bytes 3076

commit v2 on v0

v2 whole, which is shorter than its diff:
```python
import functools

import jax
import jax.numpy as jnp
import numpy as np
from jax import lax
from jax.experimental import pallas as pl
from jax.experimental.pallas import tpu as pltpu
from jax.sharding import PartitionSpec as P

AXES = ("rows", "cols")
EMPTY = -2.0
SMEM = pl.BlockSpec(memory_space=pltpu.SMEM)
VMEM = pl.BlockSpec(memory_space=pltpu.VMEM)
ANY = pl.BlockSpec(memory_space=pl.ANY)
HBM = pl.BlockSpec(memory_space=pltpu.HBM)


def layout(chips):
    if chips == 8:
        return 2, [[(0, 2), (1, 0), (2, 3), (3, 1)], [(1, 2), (3, 0)]]
    rounds = [[(c, (c + d) % chips) for c in range(chips)] for d in range(1, (chips + 1) // 2)]
    if chips % 2 == 0:
        rounds.append([(c, c + chips // 2) for c in range(chips // 2)])
    return 1, rounds


def labels(gid, size_ref, start_ref):
    label = jnp.full(gid.shape, -1, jnp.int32)
    for k in range(size_ref.shape[0]):
        first = start_ref[k]
        label = jnp.where((gid >= first) & (gid < first + size_ref[k]), k, label)
    return label


def my_block():
    return lax.axis_index("rows") * lax.axis_size("cols") + lax.axis_index("cols")


def lanes(block, rows):
    return block * rows + lax.broadcasted_iota(jnp.int32, (1, rows), 1)


def norm_kernel(size_hbm, start_hbm, live_hbm, emb_hbm, out_ref, size_ref, start_ref, live_ref, emb_ref, sems):
    pairs = ((emb_hbm, emb_ref), (size_hbm, size_ref), (start_hbm, start_ref), (live_hbm, live_ref))
    copies = [pltpu.make_async_copy(s, d, sems.at[k]) for k, (s, d) in enumerate(pairs)]
    for copy in copies:
        copy.start()
    for copy in copies:
        copy.wait()
    rows, width = emb_ref.shape
    emb = emb_ref[...]
    squares = jnp.sum(emb * emb, axis=1, keepdims=True)
    scale = lax.rsqrt(squares + 1e-06)
    member = labels(lanes(my_block(), rows), size_ref, start_ref) >= 0
    active = jnp.where(member & (live_ref[...] == 1), jnp.float32(1), jnp.float32(0))
    active = jnp.broadcast_to(active, (128, rows)).T[:, :1]
    out_ref[...] = (emb * jnp.where(active > 0, scale, jnp.float32(jnp.nan))).astype(out_ref.dtype)


def products(left, left_label, right, right_label, off=None):
    sim = lax.dot_general(left, right, (((1,), (1,)), ((), ())), preferred_element_type=jnp.float32)
    wide = jnp.concatenate([left_label] * (right_label.shape[1] // 128), axis=1)
    valid = (wide == right_label) & (sim > -1.5)
    if off is not None:
        valid = valid & off
    return jnp.where(valid, sim, jnp.float32(EMPTY))


def fold(sim):
    best = sim[:, :128]
    for c in range(128, sim.shape[1], 128):
        best = jnp.maximum(best, sim[:, c : c + 128])
    return best


def row_labels(block, rows, size_ref, start_ref):
    gid = block * rows + lax.broadcasted_iota(jnp.int32, (rows, 128), 0)
    return labels(gid, size_ref, start_ref)


def column_kernel(n, table_ref, size_ref, start_ref, *refs):
    held, out_ref = refs[:n], refs[n]
    rows = held[0].shape[0]
    me = my_block()
    own = held[0][...]
    mine = row_labels(me, rows, size_ref, start_ref)
    off = lax.broadcasted_iota(jnp.int32, (rows, rows), 0) != lax.broadcasted_iota(
        jnp.int32, (rows, rows), 1
    )
    best = jnp.full((rows, 128), EMPTY, jnp.float32)
    for k in range(n):
        keys = labels(lanes(table_ref[me, k], rows), size_ref, start_ref)
        best = jnp.maximum(best, fold(products(own, mine, held[k][...], keys, off if k == 0 else None)))
    out_ref[...] = jnp.max(best.T, axis=0, keepdims=True)


def visit_kernel(n, slot, first, table_ref, size_ref, start_ref, *refs):
    held, visitor_hbm = refs[:n], refs[n]
    before, refs = refs[n + 1 : 2 * n + 1], refs[2 * n + 1 :]
    if first:
        before = (before[0],)
    outs, back_ref, visitor, sem = refs[:n], refs[n], refs[n + 1], refs[n + 2]
    rows = held[0].shape[0]
    me = my_block()
    copy = pltpu.make_async_copy(visitor_hbm, visitor, sem)
    copy.start()
    theirs = row_labels(table_ref[me, slot], rows, size_ref, start_ref)
    copy.wait()
    best = jnp.full((rows, 128), EMPTY, jnp.float32)
    for k in range(n):
        keys = labels(lanes(table_ref[me, k], rows), size_ref, start_ref)
        sim = products(visitor[...], theirs, held[k][...], keys)
        best = jnp.maximum(best, fold(sim))
        top = jnp.max(sim, axis=0, keepdims=True)
        if k < len(before):
            top = jnp.maximum(top, before[k][...])
        outs[k][...] = top
    back_ref[...] = jnp.max(best.T, axis=0, keepdims=True)


def per_device(chips, embeddings, cluster_size, cluster_start, live):
    rows, width = embeddings.shape
    tall, rounds = layout(chips)
    total = 2 * chips
    devices = 2 * tall
    n = devices
    table = np.full((total, n + len(rounds)), -1, np.int32)
    for d in range(total):
        table[d, :n] = [d ^ k for k in range(n)]
    moves = []
    for r, sends in enumerate(rounds):
        move = [(s * devices + k, t * devices + k) for s, t in sends for k in range(devices)]
        for s, t in move:
            table[t, n + r] = s
        moves.append(move)
    table = jnp.asarray(table)
    params = pltpu.CompilerParams(vmem_limit_bytes=24 << 20)
    small = jax.ShapeDtypeStruct((1, rows), jnp.float32)

    def cost(products, blocks):
        return pl.CostEstimate(
            flops=2 * products * rows * rows * width, bytes_accessed=2 * blocks * rows * width, transcendentals=0
        )

    live = live.reshape(1, rows)
    own = pl.pallas_call(
        norm_kernel,
        out_shape=jax.ShapeDtypeStruct((rows, width), jnp.bfloat16),
        in_specs=[HBM] * 4,
        out_specs=VMEM,
        scratch_shapes=[
            pltpu.SMEM(cluster_size.shape, jnp.int32),
            pltpu.SMEM(cluster_start.shape, jnp.int32),
            pltpu.VMEM((1, rows), jnp.int32),
            pltpu.VMEM((rows, width), jnp.float32),
            pltpu.SemaphoreType.DMA((4,)),
        ],
        compiler_params=pltpu.CompilerParams(vmem_limit_bytes=60 << 20),
    )(cluster_size, cluster_start, live, embeddings)

    def swap(x, k):
        return lax.ppermute(x, AXES, [(d, d ^ k) for d in range(total)])

    visitors = [lax.ppermute(own, AXES, move) for move in moves]
    held = [own, swap(own, 1)]
    if tall == 2:
        across = swap(own, 2)
        across, first = lax.optimization_barrier((across, visitors[0]))
        visitors = [first] + visitors[1:]
        held += [across, swap(across, 1)]

    peaks = [
        pl.pallas_call(
            functools.partial(column_kernel, n),
            out_shape=small,
            in_specs=[SMEM] * 3 + [VMEM] * n,
            out_specs=VMEM,
            compiler_params=params,
            cost_estimate=cost(n, n),
        )(table, cluster_size, cluster_start, *held)
    ]
    backs = []
    for r, (visitor, move) in enumerate(zip(visitors, moves)):
        first = r == 0
        *peaks, back = pl.pallas_call(
            functools.partial(visit_kernel, n, n + r, first),
            out_shape=[small] * (n + 1),
            in_specs=[SMEM] * 3 + [VMEM] * n + [ANY] + [VMEM] * n,
            out_specs=[VMEM] * (n + 1),
            scratch_shapes=[pltpu.VMEM((rows, width), jnp.bfloat16), pltpu.SemaphoreType.DMA],
            compiler_params=params,
            cost_estimate=cost(n, n + 1),
        )(table, cluster_size, cluster_start, *held, visitor, *(peaks * n if first else peaks))
        home = [(t, s) for s, t in move]
        idle = sorted(set(range(total)) - {t for t, _ in home})
        alone = sorted(set(range(total)) - {s for _, s in home})
        backs.append(lax.ppermute(back, AXES, home + list(zip(idle, alone))))

    peak = peaks[0]
    if tall == 2:
        other = swap(jnp.concatenate([peaks[1], peaks[3]], axis=0), 1)
        peak = jnp.maximum(peak, other[:1])
        backs.append(swap(jnp.maximum(peaks[2], other[1:]), 2))
    else:
        backs.append(swap(peaks[1], 1))
    for back in backs:
        peak = jnp.maximum(peak, back)
    return jnp.where((live == 1) & (peak > -1.5), peak, jnp.float32(0.0)).reshape(rows)


def solution(mesh):
    placed = (
        P(("groups", "rows", "cols"), None),
        P("groups"),
        P("groups"),
        P(("groups", "rows", "cols")),
    )
    return jax.shard_map(
        functools.partial(per_device, mesh.shape["rows"]),
        mesh=mesh,
        in_specs=placed,
        out_specs=P(("groups", "rows", "cols")),
        check_vma=False,
    )
```

time: 87.3 us -> 40.1 us (0.46)
  blocking collectives: 23.4 us -> 0 us
  waiting for transfers between devices: 37.4 us -> 21.3 us
  between operations: 14.1 us -> 0.1 us
  starting transfers between devices: 0.01 us -> 9.62 us
  Pallas kernels: 0 us -> 7.1 us
  other arithmetic: 7.08 us -> 0.59 us
  matrix products: 5.05 us -> 0 us
  local copies, waits for them, and re-layouts: 0.02 us -> 1.1 us
    all_gather x1 -> x0, waiting for transfers between devices: 37.4 us -> none  [per_device(): lax.all_gather(normed, ('rows', 'cols'), axis=0, tiled=True)]
    all_gather x1 -> x0, blocking collectives: 23.4 us -> none  [per_device(): lax.all_gather(live, ('rows', 'cols'), axis=0, tiled=True)]
    ppermute x0 -> x9, waiting for transfers between devices: none -> 21.3 us  [the longest x2 11.2 us: per_device(): visitors = [lax.ppermute(own, AXES, move) for move in moves]]
    ppermute x0 -> x9, starting transfers between devices: none -> 9.62 us  [the longest x2 3.87 us: per_device(): visitors = [lax.ppermute(own, AXES, move) for move in moves]]
    pallas_call x0 -> x4, Pallas kernels: none -> 7.1 us  [the longest x2 3.42 us: per_device(): pl.pallas_call(functools.partial(visit_kernel, n, n + r, first), out_shap...]
    dot_general x1 -> x0, matrix products: 5.05 us -> none  [compute(): lax.dot_general(queries, keys, (((1,), (1,)), ((), ())), preferred_elemen...]
    convert_element_type x1 -> x0, other arithmetic: 2.02 us -> none  [per_device(): normed = (embeddings * lax.rsqrt(squares + 1e-06)).astype(jnp.bfloat16)]
    reduce_max x2 -> x0, other arithmetic: 1.54 us -> none  [labels_of(): return jnp.max(jnp.where(inside, ids[None, :], -1), axis=1)]
  transfers between devices with their start and end apart: 1 -> 9, of which waited for: 1 -> 7; matrix products, arithmetic and copies ran while one was open for 4% -> 0% of each run, Pallas kernels for 0% -> 8%
where the time goes in v2:
time: 40.1 us; the launch traced here: 39.9 us
  waiting for transfers between devices  21.3 us (53%)
  starting transfers between devices  9.62 us (24%)
  Pallas kernels  7.1 us (18%)
  local copies, waits for them, and re-layouts  1.1 us (3%)
  other arithmetic  0.59 us (1%)
    ppermute x2, waiting for transfers between devices, per_device(): visitors = [lax.ppermute(own, AXES, move) for move in moves]  11.2 us
    ppermute x5, waiting for transfers between devices, swap(): return lax.ppermute(x, AXES, [(d, d ^ k) for d in range(total)])  8.28 us
    ppermute x2, starting transfers between devices, per_device(): visitors = [lax.ppermute(own, AXES, move) for move in moves]  3.87 us
    ppermute x5, starting transfers between devices, swap(): return lax.ppermute(x, AXES, [(d, d ^ k) for d in range(total)])  3.68 us
    pallas_call x2, Pallas kernels, per_device(): pl.pallas_call(functools.partial(visit_kernel, n, n + r, first), out_shap...  3.42 us
    pallas_call x1, Pallas kernels, per_device(): pl.pallas_call(norm_kernel, out_shape=jax.ShapeDtypeStruct((rows, width),...  2.28 us
    ppermute x2, starting transfers between devices, per_device(): backs.append(lax.ppermute(back, AXES, home + list(zip(idle, alone))))  2.07 us
    ppermute x2, waiting for transfers between devices, per_device(): backs.append(lax.ppermute(back, AXES, home + list(zip(idle, alone))))  1.84 us
  transfers between devices with their start and end apart: 9, of which 7 were waited for; matrix products, arithmetic and copies ran while one was open for 0% of the time, Pallas kernels for 8%

profile of v2, /device:TPU:0, one launch (start us, length us, event | category | flops | bytes accessed | tf_op | source)
XLA Modules:
  0.0 39.9 jit_solution(12474328732927050739)
XLA Ops:
  0.0 0.0 copy-start.2
  0.0 0.0 copy-start.3
  0.0 2.3 %shard_map.55.refs_0_ = bf16[256,768]{1,0:T(8,128)(2,1)} custom-call(s32[4]{0:T(128)} %size_ref.5, s32[4]{0:T(128)} %start_ref.5, s32[1,256]{1,0:T(1,128)} %bitcast.2, f32[256,768]{1,0:T(8,128)} %emb_hbm.1), custom_call_target="tpu_custom_call" | custom-call | tf_op jit(solution)/shard_map/pallas_call | solution.py:147
  2.3 3.0 %collective-permute-start.1 = (bf16[256,768]{1,0:T(8,128)(2,1)}, bf16[256,768]{1,0:T(8,128)(2,1)S(1)}, u32[]{:S(2)}, u32[]{:S(2)}) collective-permute-start(bf16[256,768]{1,0:T(8,128)(2,1)} %shard_map.55.refs_0_), channel_id=1, source_target_pairs={{0,2},{1,3},{2,0},{3,1},{4,6},{5,7},{6,4},{7,5},{8,10},{9,11},{10,... | collective-permute-start | bytes 1179656 | tf_op jit(solution)/shard_map/ppermute | solution.py:163
  5.3 2.6 %collective-permute-start.2 = (bf16[256,768]{1,0:T(8,128)(2,1)}, bf16[256,768]{1,0:T(8,128)(2,1)S(1)}, u32[]{:S(2)}, u32[]{:S(2)}) collective-permute-start(bf16[256,768]{1,0:T(8,128)(2,1)} %shard_map.55.refs_0_), channel_id=1, source_target_pairs={{0,8},{1,9},{2,10},{3,11},{4,0},{5,1},{6,2},{7,3},{8,12},{9,13},{1... | collective-permute-start | bytes 1179656 | tf_op jit(solution)/shard_map/ppermute | solution.py:165
  7.9 0.0 collective-permute-start
  7.9 6.7 %collective-permute-done.1.refs_2_ = bf16[256,768]{1,0:T(8,128)(2,1)S(1)} collective-permute-done((bf16[256,768]{1,0:T(8,128)(2,1)}, bf16[256,768]{1,0:T(8,128)(2,1)S(1)}, u32[]{:S(2)}, u32[]{:S(2)}) %collective-permute-start.1) | collective-permute-done | bytes 393248 | tf_op jit(solution)/shard_map/ppermute | solution.py:163
  14.7 1.7 %collective-permute-done.2.refs_4_ = bf16[256,768]{1,0:T(8,128)(2,1)S(1)} collective-permute-done((bf16[256,768]{1,0:T(8,128)(2,1)}, bf16[256,768]{1,0:T(8,128)(2,1)S(1)}, u32[]{:S(2)}, u32[]{:S(2)}) %collective-permute-start.2) | collective-permute-done | bytes 393248 | tf_op jit(solution)/shard_map/ppermute | solution.py:165
  16.3 0.0 collective-permute-start.3
  16.3 1.3 %collective-permute-start.4 = (bf16[256,768]{1,0:T(8,128)(2,1)}, bf16[256,768]{1,0:T(8,128)(2,1)S(1)}, u32[]{:S(2)}, u32[]{:S(2)}) collective-permute-start(bf16[256,768]{1,0:T(8,128)(2,1)} %shard_map.55.refs_0_), channel_id=1, source_target_pairs={{4,8},{5,9},{6,10},{7,11},{12,0},{13,1},{14,2},{15,3},{20,24},{21,... | collective-permute-start | bytes 1179656 | tf_op jit(solution)/shard_map/ppermute | solution.py:165
  17.6 0.0 collective-permute-done.refs_1_
  17.6 0.4 %collective-permute-done.3.refs_3_ = bf16[256,768]{1,0:T(8,128)(2,1)S(1)} collective-permute-done((bf16[256,768]{1,0:T(8,128)(2,1)S(1)}, bf16[256,768]{1,0:T(8,128)(2,1)S(1)}, u32[]{:S(2)}, u32[]{:S(2)}) %collective-permute-start.3) | collective-permute-done | bytes 393248 | tf_op jit(solution)/shard_map/ppermute | solution.py:163
  18.1 0.0 copy-done.2
  18.1 0.0 copy-done.3
  18.1 0.0 copy-done.4
  18.1 0.0 copy-start
  18.1 1.0 %copy-done = bf16[256,768]{1,0:T(8,128)(2,1)S(1)} copy-done((bf16[256,768]{1,0:T(8,128)(2,1)S(1)}, bf16[256,768]{1,0:T(8,128)(2,1)}, u32[]{:S(2)}) %copy-start) | copy-done | bytes 393240
  19.1 1.4 %shard_map.56.refs_5_.refs_6_.refs_7_.refs_8_ = f32[1,256]{1,0:T(1,128)S(1)} custom-call(s32[16,6]{1,0:T(8,128)S(1)} %copy-done.2, s32[4]{0:T(128)S(1)} %copy-done.3, s32[4]{0:T(128)S(1)} %copy-done.4, bf16[256,768]{1,0:T(8,128)(2,1)S(1)} %copy-done, bf16[256,768]{1,0:T(8,128)(2,1)S(1)} %collective-permute-done.refs_1_, ...), custom_call_target="tpu_custom_call" | custom-call | flops 402653184 | bytes 1572864 | tf_op jit(solution)/shard_map/pallas_call | solution.py:174
  20.5 0.0 copy-done.1
  20.5 1.7 %shard_map.57 = (f32[1,256]{1,0:T(1,128)S(1)}, f32[1,256]{1,0:T(1,128)S(1)}, f32[1,256]{1,0:T(1,128)S(1)}, f32[1,256]{1,0:T(1,128)S(1)}, f32[1,256]{1,0:T(1,128)S(1)}) custom-call(s32[16,6]{1,0:T(8,128)S(1)} %copy-done.2, s32[4]{0:T(128)S(1)} %copy-done.3, s32[4]{0:T(128)S(1)} %copy-done.4, bf16[256,768]{1,0:T(8,128)(2,1)S(1)} %copy-done.1, ...), custom_call_target="tpu_custom_call" | custom-call | flops 402653184 | bytes 1966080 | tf_op jit(solution)/shard_map/pallas_call | solution.py:186
  22.2 9.6 %collective-permute-done.4.refs_4_ = bf16[256,768]{1,0:T(8,128)(2,1)S(1)} collective-permute-done((bf16[256,768]{1,0:T(8,128)(2,1)}, bf16[256,768]{1,0:T(8,128)(2,1)S(1)}, u32[]{:S(2)}, u32[]{:S(2)}) %collective-permute-start.4) | collective-permute-done | bytes 393248 | tf_op jit(solution)/shard_map/ppermute | solution.py:165
  31.7 1.7 %shard_map.58 = (f32[1,256]{1,0:T(1,128)S(1)}, f32[1,256]{1,0:T(1,128)S(1)}, f32[1,256]{1,0:T(1,128)S(1)}, f32[1,256]{1,0:T(1,128)S(1)}, f32[1,256]{1,0:T(1,128)S(1)}) custom-call(s32[16,6]{1,0:T(8,128)S(1)} %copy-done.2, s32[4]{0:T(128)S(1)} %copy-done.3, s32[4]{0:T(128)S(1)} %copy-done.4, bf16[256,768]{1,0:T(8,128)(2,1)S(1)} %copy-done.1, ...), custom_call_target="tpu_custom_call" | custom-call | flops 402653184 | bytes 1966080 | tf_op jit(solution)/shard_map/pallas_call | solution.py:186
  33.5 0.1 collective-permute-start.5
  33.6 0.1 collective-permute-start.7
  33.6 2.0 %collective-permute-start.6 = (f32[1,256]{1,0:T(1,128)S(1)}, f32[1,256]{1,0:T(1,128)S(1)}, u32[]{:S(2)}, u32[]{:S(2)}) collective-permute-start(f32[1,256]{1,0:T(1,128)S(1)} %get-tuple-element.26), channel_id=1, source_target_pairs={{8,0},{9,1},{10,2},{11,3},{0,4},{1,5},{2,6},{3,7},{12,8},{13,9},{1... | collective-permute-start | bytes 3080 | tf_op jit(solution)/shard_map/ppermute | solution.py:198
  35.6 0.0 collective-permute-done.5
  35.6 0.6 %collective-permute-start.8 = (f32[1,256]{1,0:T(1,128)S(1)}, f32[1,256]{1,0:T(1,128)S(1)}, u32[]{:S(2)}, u32[]{:S(2)}) collective-permute-start(f32[1,256]{1,0:T(1,128)S(1)} %slice_maximum_fusion), channel_id=1, source_target_pairs={{0,2},{1,3},{2,0},{3,1},{4,6},{5,7},{6,4},{7,5},{8,10},{9,11},{10,... | collective-permute-start | bytes 3080 | tf_op jit(solution)/shard_map/ppermute | solution.py:163
  36.2 0.1 copy-done.5
  36.3 0.9 %collective-permute-done.7 = f32[1,256]{1,0:T(1,128)S(1)} collective-permute-done((f32[1,256]{1,0:T(1,128)S(1)}, f32[1,256]{1,0:T(1,128)S(1)}, u32[]{:S(2)}, u32[]{:S(2)}) %collective-permute-start.7) | collective-permute-done | bytes 1056 | tf_op jit(solution)/shard_map/ppermute | solution.py:198
  37.2 1.0 %collective-permute-done.6 = f32[1,256]{1,0:T(1,128)S(1)} collective-permute-done((f32[1,256]{1,0:T(1,128)S(1)}, f32[1,256]{1,0:T(1,128)S(1)}, u32[]{:S(2)}, u32[]{:S(2)}) %collective-permute-start.6) | collective-permute-done | bytes 1056 | tf_op jit(solution)/shard_map/ppermute | solution.py:198
  38.2 1.1 %collective-permute-done.8 = f32[1,256]{1,0:T(1,128)S(1)} collective-permute-done((f32[1,256]{1,0:T(1,128)S(1)}, f32[1,256]{1,0:T(1,128)S(1)}, u32[]{:S(2)}, u32[]{:S(2)}) %collective-permute-start.8) | collective-permute-done | bytes 1056 | tf_op jit(solution)/shard_map/ppermute | solution.py:163
  39.3 0.6 %and_select_fusion = f32[1,256]{1,0:T(1,128)} fusion(pred[256]{0:T(512)(128)(4,1)S(1)} %broadcast_compare_fusion, f32[1,256]{1,0:T(1,128)S(1)} %collective-permute-done.8, f32[1,256]{1,0:T(1,128)S(1)} %collective-permute-done.7, f32[1,256]{1,0:T(1,128)S(1)} %collective-permute-done.6, f32[1,256]{1,0:T(1,128)S(1)} %get-tuple-element.23, ...), kind=kLoop, calls=%fused_computation | loop fusion | flops 1792 | bytes 6400 | tf_op jit(solution)/shard_map/jit(_where)/select_n | solution.py:209
  (6 shorter events, 0.0 us)
Async XLA Ops:
  0.0 18.1 %copy-start.2 = (s32[16,6]{1,0:T(8,128)S(1)}, s32[16,6]{1,0:T(8,128)}, u32[]{:S(2)}) copy-start(s32[16,6]{1,0:T(8,128)} %constant.8.clone.table_ref) | copy-start | bytes 1156
  0.0 18.1 %copy-start.3 = (s32[4]{0:T(128)S(1)}, s32[4]{0:T(128)}, u32[]{:S(2)}) copy-start(s32[4]{0:T(128)} %size_ref.5) | copy-start | bytes 52
  0.0 18.1 %copy-start.4 = (s32[4]{0:T(128)S(1)}, s32[4]{0:T(128)}, u32[]{:S(2)}) copy-start(s32[4]{0:T(128)} %start_ref.5) | copy-start | bytes 52
  2.3 12.4 %collective-permute-start.1 = (bf16[256,768]{1,0:T(8,128)(2,1)}, bf16[256,768]{1,0:T(8,128)(2,1)S(1)}, u32[]{:S(2)}, u32[]{:S(2)}) collective-permute-start(bf16[256,768]{1,0:T(8,128)(2,1)} %shard_map.55.refs_0_), channel_id=1, source_target_pairs={{0,2},{1,3},{2,0},{3,1},{4,6},{5,7},{6,4},{7,5},{8,10},{9,11},{10,... | collective-permute-start | bytes 1179656 | tf_op jit(solution)/shard_map/ppermute | solution.py:163
  5.3 11.0 %collective-permute-start.2 = (bf16[256,768]{1,0:T(8,128)(2,1)}, bf16[256,768]{1,0:T(8,128)(2,1)S(1)}, u32[]{:S(2)}, u32[]{:S(2)}) collective-permute-start(bf16[256,768]{1,0:T(8,128)(2,1)} %shard_map.55.refs_0_), channel_id=1, source_target_pairs={{0,8},{1,9},{2,10},{3,11},{4,0},{5,1},{6,2},{7,3},{8,12},{9,13},{1... | collective-permute-start | bytes 1179656 | tf_op jit(solution)/shard_map/ppermute | solution.py:165
  7.9 9.7 %collective-permute-start = (bf16[256,768]{1,0:T(8,128)(2,1)}, bf16[256,768]{1,0:T(8,128)(2,1)S(1)}, u32[]{:S(2)}, u32[]{:S(2)}) collective-permute-start(bf16[256,768]{1,0:T(8,128)(2,1)} %shard_map.55.refs_0_), channel_id=1, source_target_pairs={{0,1},{1,0},{2,3},{3,2},{4,5},{5,4},{6,7},{7,6},{8,9},{9,8},{10,11... | collective-permute-start | bytes 1179656 | tf_op jit(solution)/shard_map/ppermute | solution.py:163
  16.3 1.7 %collective-permute-start.3 = (bf16[256,768]{1,0:T(8,128)(2,1)S(1)}, bf16[256,768]{1,0:T(8,128)(2,1)S(1)}, u32[]{:S(2)}, u32[]{:S(2)}) collective-permute-start(bf16[256,768]{1,0:T(8,128)(2,1)S(1)} %collective-permute-done.1.refs_2_), channel_id=1, source_target_pairs={{0,1},{1,0},{2,3},{3,2},{4,5},{5,4},{6,7},{7,6},{8,9},{9,8},{10,11... | collective-permute-start | bytes 1179656 | tf_op jit(solution)/shard_map/ppermute | solution.py:163
  16.3 15.4 %collective-permute-start.4 = (bf16[256,768]{1,0:T(8,128)(2,1)}, bf16[256,768]{1,0:T(8,128)(2,1)S(1)}, u32[]{:S(2)}, u32[]{:S(2)}) collective-permute-start(bf16[256,768]{1,0:T(8,128)(2,1)} %shard_map.55.refs_0_), channel_id=1, source_target_pairs={{4,8},{5,9},{6,10},{7,11},{12,0},{13,1},{14,2},{15,3},{20,24},{21,... | collective-permute-start | bytes 1179656 | tf_op jit(solution)/shard_map/ppermute | solution.py:165
  18.1 1.0 %copy-start = (bf16[256,768]{1,0:T(8,128)(2,1)S(1)}, bf16[256,768]{1,0:T(8,128)(2,1)}, u32[]{:S(2)}) copy-start(bf16[256,768]{1,0:T(8,128)(2,1)} %shard_map.55.refs_0_) | copy-start | bytes 1179652
  19.1 1.4 %copy-start.1 = (bf16[256,768]{1,0:T(8,128)(2,1)S(1)}, bf16[256,768]{1,0:T(8,128)(2,1)}, u32[]{:S(2)}) copy-start(bf16[256,768]{1,0:T(8,128)(2,1)} %shard_map.55.refs_0_) | copy-start | bytes 1179652
  33.5 2.2 %collective-permute-start.5 = (f32[2,256]{1,0:T(2,128)S(1)}, f32[2,256]{1,0:T(2,128)S(1)}, u32[]{:S(2)}, u32[]{:S(2)}) collective-permute-start(f32[2,256]{1,0:T(2,128)S(1)} %pad_maximum_fusion), channel_id=1, source_target_pairs={{0,1},{1,0},{2,3},{3,2},{4,5},{5,4},{6,7},{7,6},{8,9},{9,8},{10,11... | collective-permute-start | bytes 6152 | tf_op jit(solution)/shard_map/ppermute | solution.py:163
  33.6 3.6 %collective-permute-start.7 = (f32[1,256]{1,0:T(1,128)S(1)}, f32[1,256]{1,0:T(1,128)S(1)}, u32[]{:S(2)}, u32[]{:S(2)}) collective-permute-start(f32[1,256]{1,0:T(1,128)S(1)} %get-tuple-element.27), channel_id=1, source_target_pairs={{8,4},{9,5},{10,6},{11,7},{0,12},{1,13},{2,14},{3,15},{4,0},{5,1},... | collective-permute-start | bytes 3080 | tf_op jit(solution)/shard_map/ppermute | solution.py:198
  33.6 4.5 %collective-permute-start.6 = (f32[1,256]{1,0:T(1,128)S(1)}, f32[1,256]{1,0:T(1,128)S(1)}, u32[]{:S(2)}, u32[]{:S(2)}) collective-permute-start(f32[1,256]{1,0:T(1,128)S(1)} %get-tuple-element.26), channel_id=1, source_target_pairs={{8,0},{9,1},{10,2},{11,3},{0,4},{1,5},{2,6},{3,7},{12,8},{13,9},{1... | collective-permute-start | bytes 3080 | tf_op jit(solution)/shard_map/ppermute | solution.py:198
  35.6 0.7 %copy-start.5 = (s32[256]{0:T(256)S(1)}, s32[256]{0:T(256)}, u32[]{:S(2)}) copy-start(s32[256]{0:T(256)} %param.8) | copy-start | bytes 3076
  35.6 3.6 %collective-permute-start.8 = (f32[1,256]{1,0:T(1,128)S(1)}, f32[1,256]{1,0:T(1,128)S(1)}, u32[]{:S(2)}, u32[]{:S(2)}) collective-permute-start(f32[1,256]{1,0:T(1,128)S(1)} %slice_maximum_fusion), channel_id=1, source_target_pairs={{0,2},{1,3},{2,0},{3,1},{4,6},{5,7},{6,4},{7,5},{8,10},{9,11},{10,... | collective-permute-start | bytes 3080 | tf_op jit(solution)/shard_map/ppermute | solution.py:163

commit v3 on v2

--- a/solution.py
+++ b/solution.py
@@ -79,8 +79,13 @@
     return labels(gid, size_ref, start_ref)
 
 
-def column_kernel(n, table_ref, size_ref, start_ref, *refs):
-    held, out_ref = refs[:n], refs[n]
+def blocks_of(refs):
+    return [refs[0], refs[1]] + [refs[2].at[lax.axis_index("cols") ^ k] for k in range(2) if len(refs) > 2]
+
+
+def column_kernel(table_ref, size_ref, start_ref, *refs):
+    held, out_ref = blocks_of(refs[:-1]), refs[-1]
+    n = len(held)
     rows = held[0].shape[0]
     me = my_block()
     own = held[0][...]
@@ -96,8 +101,9 @@
 
 
 def visit_kernel(n, slot, first, table_ref, size_ref, start_ref, *refs):
-    held, visitor_hbm = refs[:n], refs[n]
-    before, refs = refs[n + 1 : 2 * n + 1], refs[2 * n + 1 :]
+    arrays = 2 if n == 2 else 3
+    held, visitor_hbm, refs = blocks_of(refs[:arrays]), refs[arrays], refs[arrays + 1 :]
+    before, refs = refs[:n], refs[n:]
     if first:
         before = (before[0],)
     outs, back_ref, visitor, sem = refs[:n], refs[n], refs[n + 1], refs[n + 2]
@@ -156,7 +162,7 @@
             pltpu.VMEM((rows, width), jnp.float32),
             pltpu.SemaphoreType.DMA((4,)),
         ],
-        compiler_params=pltpu.CompilerParams(vmem_limit_bytes=60 << 20),
+        compiler_params=pltpu.CompilerParams(vmem_limit_bytes=(63 << 20) + (512 << 10)),
     )(cluster_size, cluster_start, live, embeddings)
 
     def swap(x, k):
@@ -165,16 +171,13 @@
     visitors = [lax.ppermute(own, AXES, move) for move in moves]
     held = [own, swap(own, 1)]
     if tall == 2:
-        across = swap(own, 2)
-        across, first = lax.optimization_barrier((across, visitors[0]))
-        visitors = [first] + visitors[1:]
-        held += [across, swap(across, 1)]
+        held.append(lax.all_gather(swap(own, 2), "cols"))
 
     peaks = [
         pl.pallas_call(
-            functools.partial(column_kernel, n),
+            column_kernel,
             out_shape=small,
-            in_specs=[SMEM] * 3 + [VMEM] * n,
+            in_specs=[SMEM] * 3 + [VMEM] * len(held),
             out_specs=VMEM,
             compiler_params=params,
             cost_estimate=cost(n, n),
@@ -186,7 +189,7 @@
         *peaks, back = pl.pallas_call(
             functools.partial(visit_kernel, n, n + r, first),
             out_shape=[small] * (n + 1),
-            in_specs=[SMEM] * 3 + [VMEM] * n + [ANY] + [VMEM] * n,
+            in_specs=[SMEM] * 3 + [VMEM] * len(held) + [ANY] + [VMEM] * n,
             out_specs=[VMEM] * (n + 1),
             scratch_shapes=[pltpu.VMEM((rows, width), jnp.bfloat16), pltpu.SemaphoreType.DMA],
             compiler_params=params,

time: 40.1 us -> 35.7 us (0.89)
  waiting for transfers between devices: 21.3 us -> 15 us
  blocking collectives: 0 us -> 2.36 us
    ppermute x2, waiting for transfers between devices: 11.2 us -> 6.6 us  [per_device(): visitors = [lax.ppermute(own, AXES, move) for move in moves]]
    all_gather x0 -> x1, blocking collectives: none -> 2.36 us  [per_device(): held.append(lax.all_gather(swap(own, 2), 'cols'))]
    ppermute x5 -> x4, waiting for transfers between devices: 8.28 us -> 6.57 us  [swap(): return lax.ppermute(x, AXES, [(d, d ^ k) for d in range(total)])]
    unnamed x12 -> x10, local copies, waits for them, and re-layouts: 1.1 us -> 0.76 us
    ppermute x5 -> x4, starting transfers between devices: 3.68 us -> 3.68 us  [swap(): return lax.ppermute(x, AXES, [(d, d ^ k) for d in range(total)])]
  transfers between devices with their start and end apart: 9 -> 8, of which waited for: 7 -> 5; matrix products, arithmetic and copies ran while one was open for 0% -> 0% of each run, Pallas kernels for 8% -> 9%
where the time goes in v3:
time: 35.7 us; the launch traced here: 35.5 us
  waiting for transfers between devices  15 us (42%)
  starting transfers between devices  9.62 us (27%)
  Pallas kernels  7.03 us (20%)
  blocking collectives  2.36 us (7%)
  local copies, waits for them, and re-layouts  0.76 us (2%)
  other arithmetic  0.59 us (2%)
    ppermute x2, waiting for transfers between devices, per_device(): visitors = [lax.ppermute(own, AXES, move) for move in moves]  6.6 us
    ppermute x4, waiting for transfers between devices, swap(): return lax.ppermute(x, AXES, [(d, d ^ k) for d in range(total)])  6.57 us
    ppermute x2, starting transfers between devices, per_device(): visitors = [lax.ppermute(own, AXES, move) for move in moves]  3.87 us
    ppermute x4, starting transfers between devices, swap(): return lax.ppermute(x, AXES, [(d, d ^ k) for d in range(total)])  3.68 us
    pallas_call x2, Pallas kernels, per_device(): pl.pallas_call(functools.partial(visit_kernel, n, n + r, first), out_shap...  3.41 us
    all_gather x1, blocking collectives, per_device(): held.append(lax.all_gather(swap(own, 2), 'cols'))  2.36 us
    pallas_call x1, Pallas kernels, per_device(): pl.pallas_call(norm_kernel, out_shape=jax.ShapeDtypeStruct((rows, width),...  2.22 us
    ppermute x2, starting transfers between devices, per_device(): backs.append(lax.ppermute(back, AXES, home + list(zip(idle, alone))))  2.07 us
  transfers between devices with their start and end apart: 8, of which 5 were waited for; matrix products, arithmetic and copies ran while one was open for 0% of the time, Pallas kernels for 9%

profile of v3, /device:TPU:0, one launch (start us, length us, event | category | flops | bytes accessed | tf_op | source)
XLA Modules:
  0.0 35.5 jit_solution(1698463664613240074)
XLA Ops:
  0.0 2.2 %shard_map.55.refs_0_ = bf16[256,768]{1,0:T(8,128)(2,1)} custom-call(s32[4]{0:T(128)} %size_ref.5, s32[4]{0:T(128)} %start_ref.5, s32[1,256]{1,0:T(1,128)} %bitcast.6, f32[256,768]{1,0:T(8,128)} %emb_hbm.1), custom_call_target="tpu_custom_call" | custom-call | tf_op jit(solution)/shard_map/pallas_call | solution.py:153
  2.2 0.0 copy-start
  2.2 0.0 copy-start.1
  2.3 3.0 %collective-permute-start.1 = (bf16[256,768]{1,0:T(8,128)(2,1)}, bf16[256,768]{1,0:T(8,128)(2,1)S(1)}, u32[]{:S(2)}, u32[]{:S(2)}) collective-permute-start(bf16[256,768]{1,0:T(8,128)(2,1)} %shard_map.55.refs_0_), channel_id=1, source_target_pairs={{0,2},{1,3},{2,0},{3,1},{4,6},{5,7},{6,4},{7,5},{8,10},{9,11},{10,... | collective-permute-start | bytes 1179656 | tf_op jit(solution)/shard_map/ppermute | solution.py:169
  5.3 0.0 collective-permute-start
  5.3 2.6 %collective-permute-start.3 = (bf16[256,768]{1,0:T(8,128)(2,1)}, bf16[256,768]{1,0:T(8,128)(2,1)S(1)}, u32[]{:S(2)}, u32[]{:S(2)}) collective-permute-start(bf16[256,768]{1,0:T(8,128)(2,1)} %shard_map.55.refs_0_), channel_id=1, source_target_pairs={{0,8},{1,9},{2,10},{3,11},{4,0},{5,1},{6,2},{7,3},{8,12},{9,13},{1... | collective-permute-start | bytes 1179656 | tf_op jit(solution)/shard_map/ppermute | solution.py:171
  7.9 1.3 %collective-permute-start.2 = (bf16[256,768]{1,0:T(8,128)(2,1)}, bf16[256,768]{1,0:T(8,128)(2,1)S(1)}, u32[]{:S(2)}, u32[]{:S(2)}) collective-permute-start(bf16[256,768]{1,0:T(8,128)(2,1)} %shard_map.55.refs_0_), channel_id=1, source_target_pairs={{4,8},{5,9},{6,10},{7,11},{12,0},{13,1},{14,2},{15,3},{20,24},{21,... | collective-permute-start | bytes 1179656 | tf_op jit(solution)/shard_map/ppermute | solution.py:171
  9.2 5.4 %collective-permute-done.1 = bf16[256,768]{1,0:T(8,128)(2,1)S(1)} collective-permute-done((bf16[256,768]{1,0:T(8,128)(2,1)}, bf16[256,768]{1,0:T(8,128)(2,1)S(1)}, u32[]{:S(2)}, u32[]{:S(2)}) %collective-permute-start.1) | collective-permute-done | bytes 393248 | tf_op jit(solution)/shard_map/ppermute | solution.py:169
  14.6 2.4 %all-gather = bf16[512,768]{1,0:T(8,128)(2,1)S(1)} all-gather(bf16[256,768]{1,0:T(8,128)(2,1)S(1)} %collective-permute-done.1), channel_id=2, replica_groups=mesh['groups'=2,'rows'=8,'cols'=2] {'cols'}, dimensions={0}, use_global_device_ids=true | all-gather | bytes 1179648 | tf_op jit(solution)/shard_map/all_gather | solution.py:174
  17.0 0.0 copy-start.2
  17.0 0.0 copy-start.3
  17.0 0.0 collective-permute-done.refs_1_
  17.0 0.0 copy-done
  17.0 0.0 copy-done.1
  17.0 0.6 %copy-done.2 = s32[4]{0:T(128)S(1)} copy-done((s32[4]{0:T(128)S(1)}, s32[4]{0:T(128)}, u32[]{:S(2)}) %copy-start.2) | copy-done | bytes 40
  17.6 0.0 copy-done.3
  17.6 1.4 %shard_map.56.refs_4_.refs_5_.refs_6_.refs_7_ = f32[1,256]{1,0:T(1,128)S(1)} custom-call(s32[16,6]{1,0:T(8,128)S(1)} %copy-done.1, s32[4]{0:T(128)S(1)} %copy-done.2, s32[4]{0:T(128)S(1)} %copy-done.3, bf16[256,768]{1,0:T(8,128)(2,1)S(1)} %copy-done, bf16[256,768]{1,0:T(8,128)(2,1)S(1)} %collective-permute-done.refs_1_, bf16[2,256,768]{2,1,0:T(8,128)(2,1)S(1)} %bitcast.3), custom_call_target="tpu_custom_call" | custom-call | flops 402653184 | bytes 1572864 | tf_op jit(solution)/shard_map/pallas_call | solution.py:177
  19.0 0.0 collective-permute-done.3.refs_3_
  19.1 1.7 %shard_map.57 = (f32[1,256]{1,0:T(1,128)S(1)}, f32[1,256]{1,0:T(1,128)S(1)}, f32[1,256]{1,0:T(1,128)S(1)}, f32[1,256]{1,0:T(1,128)S(1)}, f32[1,256]{1,0:T(1,128)S(1)}) custom-call(s32[16,6]{1,0:T(8,128)S(1)} %copy-done.1, s32[4]{0:T(128)S(1)} %copy-done.2, s32[4]{0:T(128)S(1)} %copy-done.3, bf16[256,768]{1,0:T(8,128)(2,1)S(1)} %copy-done, ...), custom_call_target="tpu_custom_call" | custom-call | flops 402653184 | bytes 1966080 | tf_op jit(solution)/shard_map/pallas_call | solution.py:189
  20.8 6.6 %collective-permute-done.2.refs_3_ = bf16[256,768]{1,0:T(8,128)(2,1)S(1)} collective-permute-done((bf16[256,768]{1,0:T(8,128)(2,1)}, bf16[256,768]{1,0:T(8,128)(2,1)S(1)}, u32[]{:S(2)}, u32[]{:S(2)}) %collective-permute-start.2) | collective-permute-done | bytes 393248 | tf_op jit(solution)/shard_map/ppermute | solution.py:171
  27.4 1.7 %shard_map.58 = (f32[1,256]{1,0:T(1,128)S(1)}, f32[1,256]{1,0:T(1,128)S(1)}, f32[1,256]{1,0:T(1,128)S(1)}, f32[1,256]{1,0:T(1,128)S(1)}, f32[1,256]{1,0:T(1,128)S(1)}) custom-call(s32[16,6]{1,0:T(8,128)S(1)} %copy-done.1, s32[4]{0:T(128)S(1)} %copy-done.2, s32[4]{0:T(128)S(1)} %copy-done.3, bf16[256,768]{1,0:T(8,128)(2,1)S(1)} %copy-done, ...), custom_call_target="tpu_custom_call" | custom-call | flops 402653184 | bytes 1966080 | tf_op jit(solution)/shard_map/pallas_call | solution.py:189
  29.1 0.1 collective-permute-start.4
  29.2 0.1 collective-permute-start.6
  29.2 2.0 %collective-permute-start.5 = (f32[1,256]{1,0:T(1,128)S(1)}, f32[1,256]{1,0:T(1,128)S(1)}, u32[]{:S(2)}, u32[]{:S(2)}) collective-permute-start(f32[1,256]{1,0:T(1,128)S(1)} %get-tuple-element.22), channel_id=1, source_target_pairs={{8,0},{9,1},{10,2},{11,3},{0,4},{1,5},{2,6},{3,7},{12,8},{13,9},{1... | collective-permute-start | bytes 3080 | tf_op jit(solution)/shard_map/ppermute | solution.py:201
  31.2 0.0 collective-permute-done.4
  31.2 0.0 copy-start.4
  31.3 0.6 %collective-permute-start.7 = (f32[1,256]{1,0:T(1,128)S(1)}, f32[1,256]{1,0:T(1,128)S(1)}, u32[]{:S(2)}, u32[]{:S(2)}) collective-permute-start(f32[1,256]{1,0:T(1,128)S(1)} %slice_maximum_fusion), channel_id=1, source_target_pairs={{0,2},{1,3},{2,0},{3,1},{4,6},{5,7},{6,4},{7,5},{8,10},{9,11},{10,... | collective-permute-start | bytes 3080 | tf_op jit(solution)/shard_map/ppermute | solution.py:169
  31.8 0.1 copy-done.4
  31.9 0.9 %collective-permute-done.6 = f32[1,256]{1,0:T(1,128)S(1)} collective-permute-done((f32[1,256]{1,0:T(1,128)S(1)}, f32[1,256]{1,0:T(1,128)S(1)}, u32[]{:S(2)}, u32[]{:S(2)}) %collective-permute-start.6) | collective-permute-done | bytes 1056 | tf_op jit(solution)/shard_map/ppermute | solution.py:201
  32.8 1.0 %collective-permute-done.5 = f32[1,256]{1,0:T(1,128)S(1)} collective-permute-done((f32[1,256]{1,0:T(1,128)S(1)}, f32[1,256]{1,0:T(1,128)S(1)}, u32[]{:S(2)}, u32[]{:S(2)}) %collective-permute-start.5) | collective-permute-done | bytes 1056 | tf_op jit(solution)/shard_map/ppermute | solution.py:201
  33.8 1.1 %collective-permute-done.7 = f32[1,256]{1,0:T(1,128)S(1)} collective-permute-done((f32[1,256]{1,0:T(1,128)S(1)}, f32[1,256]{1,0:T(1,128)S(1)}, u32[]{:S(2)}, u32[]{:S(2)}) %collective-permute-start.7) | collective-permute-done | bytes 1056 | tf_op jit(solution)/shard_map/ppermute | solution.py:169
  34.9 0.6 %and_select_fusion = f32[1,256]{1,0:T(1,128)} fusion(pred[256]{0:T(512)(128)(4,1)S(1)} %broadcast_compare_fusion, f32[1,256]{1,0:T(1,128)S(1)} %collective-permute-done.7, f32[1,256]{1,0:T(1,128)S(1)} %collective-permute-done.6, f32[1,256]{1,0:T(1,128)S(1)} %collective-permute-done.5, f32[1,256]{1,0:T(1,128)S(1)} %get-tuple-element.19, ...), kind=kLoop, calls=%fused_computation | loop fusion | flops 1792 | bytes 6400 | tf_op jit(solution)/shard_map/jit(_where)/select_n | solution.py:212
  (3 shorter events, 0.0 us)
Async XLA Ops:
  2.2 14.7 %copy-start = (bf16[256,768]{1,0:T(8,128)(2,1)S(1)}, bf16[256,768]{1,0:T(8,128)(2,1)}, u32[]{:S(2)}) copy-start(bf16[256,768]{1,0:T(8,128)(2,1)} %shard_map.55.refs_0_) | copy-start | bytes 1179652
  2.2 14.7 %copy-start.1 = (s32[16,6]{1,0:T(8,128)S(1)}, s32[16,6]{1,0:T(8,128)}, u32[]{:S(2)}) copy-start(s32[16,6]{1,0:T(8,128)} %constant.8.clone.table_ref) | copy-start | bytes 1156
  2.3 12.4 %collective-permute-start.1 = (bf16[256,768]{1,0:T(8,128)(2,1)}, bf16[256,768]{1,0:T(8,128)(2,1)S(1)}, u32[]{:S(2)}, u32[]{:S(2)}) collective-permute-start(bf16[256,768]{1,0:T(8,128)(2,1)} %shard_map.55.refs_0_), channel_id=1, source_target_pairs={{0,2},{1,3},{2,0},{3,1},{4,6},{5,7},{6,4},{7,5},{8,10},{9,11},{10,... | collective-permute-start | bytes 1179656 | tf_op jit(solution)/shard_map/ppermute | solution.py:169
  5.3 11.7 %collective-permute-start = (bf16[256,768]{1,0:T(8,128)(2,1)}, bf16[256,768]{1,0:T(8,128)(2,1)S(1)}, u32[]{:S(2)}, u32[]{:S(2)}) collective-permute-start(bf16[256,768]{1,0:T(8,128)(2,1)} %shard_map.55.refs_0_), channel_id=1, source_target_pairs={{0,1},{1,0},{2,3},{3,2},{4,5},{5,4},{6,7},{7,6},{8,9},{9,8},{10,11... | collective-permute-start | bytes 1179656 | tf_op jit(solution)/shard_map/ppermute | solution.py:169
  5.3 13.8 %collective-permute-start.3 = (bf16[256,768]{1,0:T(8,128)(2,1)}, bf16[256,768]{1,0:T(8,128)(2,1)S(1)}, u32[]{:S(2)}, u32[]{:S(2)}) collective-permute-start(bf16[256,768]{1,0:T(8,128)(2,1)} %shard_map.55.refs_0_), channel_id=1, source_target_pairs={{0,8},{1,9},{2,10},{3,11},{4,0},{5,1},{6,2},{7,3},{8,12},{9,13},{1... | collective-permute-start | bytes 1179656 | tf_op jit(solution)/shard_map/ppermute | solution.py:171
  7.9 19.5 %collective-permute-start.2 = (bf16[256,768]{1,0:T(8,128)(2,1)}, bf16[256,768]{1,0:T(8,128)(2,1)S(1)}, u32[]{:S(2)}, u32[]{:S(2)}) collective-permute-start(bf16[256,768]{1,0:T(8,128)(2,1)} %shard_map.55.refs_0_), channel_id=1, source_target_pairs={{4,8},{5,9},{6,10},{7,11},{12,0},{13,1},{14,2},{15,3},{20,24},{21,... | collective-permute-start | bytes 1179656 | tf_op jit(solution)/shard_map/ppermute | solution.py:171
  17.0 0.7 %copy-start.2 = (s32[4]{0:T(128)S(1)}, s32[4]{0:T(128)}, u32[]{:S(2)}) copy-start(s32[4]{0:T(128)} %size_ref.5) | copy-start | bytes 52
  17.0 0.7 %copy-start.3 = (s32[4]{0:T(128)S(1)}, s32[4]{0:T(128)}, u32[]{:S(2)}) copy-start(s32[4]{0:T(128)} %start_ref.5) | copy-start | bytes 52
  29.1 2.2 %collective-permute-start.4 = (f32[2,256]{1,0:T(2,128)S(1)}, f32[2,256]{1,0:T(2,128)S(1)}, u32[]{:S(2)}, u32[]{:S(2)}) collective-permute-start(f32[2,256]{1,0:T(2,128)S(1)} %pad_maximum_fusion), channel_id=1, source_target_pairs={{0,1},{1,0},{2,3},{3,2},{4,5},{5,4},{6,7},{7,6},{8,9},{9,8},{10,11... | collective-permute-start | bytes 6152 | tf_op jit(solution)/shard_map/ppermute | solution.py:169
  29.2 3.6 %collective-permute-start.6 = (f32[1,256]{1,0:T(1,128)S(1)}, f32[1,256]{1,0:T(1,128)S(1)}, u32[]{:S(2)}, u32[]{:S(2)}) collective-permute-start(f32[1,256]{1,0:T(1,128)S(1)} %get-tuple-element.23), channel_id=1, source_target_pairs={{8,4},{9,5},{10,6},{11,7},{0,12},{1,13},{2,14},{3,15},{4,0},{5,1},... | collective-permute-start | bytes 3080 | tf_op jit(solution)/shard_map/ppermute | solution.py:201
  29.2 4.5 %collective-permute-start.5 = (f32[1,256]{1,0:T(1,128)S(1)}, f32[1,256]{1,0:T(1,128)S(1)}, u32[]{:S(2)}, u32[]{:S(2)}) collective-permute-start(f32[1,256]{1,0:T(1,128)S(1)} %get-tuple-element.22), channel_id=1, source_target_pairs={{8,0},{9,1},{10,2},{11,3},{0,4},{1,5},{2,6},{3,7},{12,8},{13,9},{1... | collective-permute-start | bytes 3080 | tf_op jit(solution)/shard_map/ppermute | solution.py:201
  31.2 0.7 %copy-start.4 = (s32[256]{0:T(256)S(1)}, s32[256]{0:T(256)}, u32[]{:S(2)}) copy-start(s32[256]{0:T(256)} %param.8) | copy-start | bytes 3076
  31.3 3.6 %collective-permute-start.7 = (f32[1,256]{1,0:T(1,128)S(1)}, f32[1,256]{1,0:T(1,128)S(1)}, u32[]{:S(2)}, u32[]{:S(2)}) collective-permute-start(f32[1,256]{1,0:T(1,128)S(1)} %slice_maximum_fusion), channel_id=1, source_target_pairs={{0,2},{1,3},{2,0},{3,1},{4,6},{5,7},{6,4},{7,5},{8,10},{9,11},{10,... | collective-permute-start | bytes 3080 | tf_op jit(solution)/shard_map/ppermute | solution.py:169

commit v4 on v3

--- a/solution.py
+++ b/solution.py
@@ -12,7 +12,6 @@
 EMPTY = -2.0
 SMEM = pl.BlockSpec(memory_space=pltpu.SMEM)
 VMEM = pl.BlockSpec(memory_space=pltpu.VMEM)
-ANY = pl.BlockSpec(memory_space=pl.ANY)
 HBM = pl.BlockSpec(memory_space=pltpu.HBM)
 
 
@@ -80,10 +79,16 @@
 
 
 def blocks_of(refs):
-    return [refs[0], refs[1]] + [refs[2].at[lax.axis_index("cols") ^ k] for k in range(2) if len(refs) > 2]
-
-
-def column_kernel(table_ref, size_ref, start_ref, *refs):
+    blocks = []
+    for ref in refs:
+        if len(ref.shape) == 2:
+            blocks.append(ref)
+        else:
+            blocks += [ref.at[lax.axis_index("cols") ^ k] for k in range(2)]
+    return blocks
+
+
+def column_kernel(table_ref, size_ref, start_ref, before_ref, *refs):
     held, out_ref = blocks_of(refs[:-1]), refs[-1]
     n = len(held)
     rows = held[0].shape[0]
@@ -97,31 +102,23 @@
     for k in range(n):
         keys = labels(lanes(table_ref[me, k], rows), size_ref, start_ref)
         best = jnp.maximum(best, fold(products(own, mine, held[k][...], keys, off if k == 0 else None)))
-    out_ref[...] = jnp.max(best.T, axis=0, keepdims=True)
-
-
-def visit_kernel(n, slot, first, table_ref, size_ref, start_ref, *refs):
-    arrays = 2 if n == 2 else 3
-    held, visitor_hbm, refs = blocks_of(refs[:arrays]), refs[arrays], refs[arrays + 1 :]
-    before, refs = refs[:n], refs[n:]
-    if first:
-        before = (before[0],)
-    outs, back_ref, visitor, sem = refs[:n], refs[n], refs[n + 1], refs[n + 2]
-    rows = held[0].shape[0]
+    out_ref[...] = jnp.maximum(before_ref[...], jnp.max(best.T, axis=0, keepdims=True))
+
+
+def visit_kernel(ids, slot, blocks, befores, table_ref, size_ref, start_ref, visitor, *refs):
+    n = len(ids)
+    held, refs = blocks_of(refs[:blocks]), refs[blocks:]
+    before, (*outs, back_ref) = refs[:befores], refs[befores:]
+    rows = visitor.shape[0]
     me = my_block()
-    copy = pltpu.make_async_copy(visitor_hbm, visitor, sem)
-    copy.start()
     theirs = row_labels(table_ref[me, slot], rows, size_ref, start_ref)
-    copy.wait()
     best = jnp.full((rows, 128), EMPTY, jnp.float32)
     for k in range(n):
-        keys = labels(lanes(table_ref[me, k], rows), size_ref, start_ref)
+        keys = labels(lanes(table_ref[me, ids[k]], rows), size_ref, start_ref)
         sim = products(visitor[...], theirs, held[k][...], keys)
         best = jnp.maximum(best, fold(sim))
         top = jnp.max(sim, axis=0, keepdims=True)
-        if k < len(before):
-            top = jnp.maximum(top, before[k][...])
-        outs[k][...] = top
+        outs[k][...] = jnp.maximum(top, before[k][...]) if befores else top
     back_ref[...] = jnp.max(best.T, axis=0, keepdims=True)
 
 
@@ -169,32 +166,37 @@
         return lax.ppermute(x, AXES, [(d, d ^ k) for d in range(total)])
 
     visitors = [lax.ppermute(own, AXES, move) for move in moves]
+    def visit(r, ids, held, before):
+        *peaks, back = pl.pallas_call(
+            functools.partial(visit_kernel, ids, n + r, len(held), len(before)),
+            out_shape=[small] * (len(ids) + 1),
+            in_specs=[SMEM] * 3 + [VMEM] * (1 + len(held) + len(before)),
+            out_specs=[VMEM] * (len(ids) + 1),
+            compiler_params=params,
+            cost_estimate=cost(len(ids), len(ids) + 1),
+        )(table, cluster_size, cluster_start, visitors[r], *held, *before)
+        return peaks, back
+
     held = [own, swap(own, 1)]
+    peaks, back = visit(0, (0, 1), held, [])
     if tall == 2:
-        held.append(lax.all_gather(swap(own, 2), "cols"))
-
-    peaks = [
-        pl.pallas_call(
-            column_kernel,
-            out_shape=small,
-            in_specs=[SMEM] * 3 + [VMEM] * len(held),
-            out_specs=VMEM,
-            compiler_params=params,
-            cost_estimate=cost(n, n),
-        )(table, cluster_size, cluster_start, *held)
-    ]
+        across, *peaks = lax.optimization_barrier((swap(own, 2), *peaks))
+        held.append(lax.all_gather(across, "cols"))
+        more, rest = visit(0, (2, 3), held[2:], [])
+        peaks, back = peaks + more, jnp.maximum(back, rest)
+
+    peaks[0] = pl.pallas_call(
+        column_kernel,
+        out_shape=small,
+        in_specs=[SMEM] * 3 + [VMEM] * (1 + len(held)),
+        out_specs=VMEM,
+        compiler_params=params,
+        cost_estimate=cost(n, n),
+    )(table, cluster_size, cluster_start, peaks[0], *held)
     backs = []
-    for r, (visitor, move) in enumerate(zip(visitors, moves)):
-        first = r == 0
-        *peaks, back = pl.pallas_call(
-            functools.partial(visit_kernel, n, n + r, first),
-            out_shape=[small] * (n + 1),
-            in_specs=[SMEM] * 3 + [VMEM] * len(held) + [ANY] + [VMEM] * n,
-            out_specs=[VMEM] * (n + 1),
-            scratch_shapes=[pltpu.VMEM((rows, width), jnp.bfloat16), pltpu.SemaphoreType.DMA],
-            compiler_params=params,
-            cost_estimate=cost(n, n + 1),
-        )(table, cluster_size, cluster_start, *held, visitor, *(peaks * n if first else peaks))
+    for r, move in enumerate(moves):
+        if r:
+            peaks, back = visit(r, tuple(range(n)), held, peaks)
         home = [(t, s) for s, t in move]
         idle = sorted(set(range(total)) - {t for t, _ in home})
         alone = sorted(set(range(total)) - {s for _, s in home})
@@ -209,7 +211,7 @@
         backs.append(swap(peaks[1], 1))
     for back in backs:
         peak = jnp.maximum(peak, back)
-    return jnp.where((live == 1) & (peak > -1.5), peak, jnp.float32(0.0)).reshape(rows)
+    return jnp.where(peak > -1.5, peak, jnp.float32(0.0)).reshape(rows)
 
 
 def solution(mesh):

time: 35.7 us -> 34.1 us (0.955)
  waiting for transfers between devices: 15 us -> 10.8 us
  starting transfers between devices: 9.62 us -> 11.6 us
  Pallas kernels: 7.03 us -> 7.5 us
    ppermute x4, waiting for transfers between devices: 6.57 us -> 2.82 us  [swap(): return lax.ppermute(x, AXES, [(d, d ^ k) for d in range(total)])]
    ppermute x2, waiting for transfers between devices: 1.84 us -> 0.01 us  [per_device(): backs.append(lax.ppermute(back, AXES, home + list(zip(idle, alone))))]
    ppermute x2, starting transfers between devices: 3.87 us -> 5.37 us  [per_device(): visitors = [lax.ppermute(own, AXES, move) for move in moves]]
    ppermute x2, waiting for transfers between devices: 6.6 us -> 7.99 us  [per_device(): visitors = [lax.ppermute(own, AXES, move) for move in moves]]
    ppermute x2, starting transfers between devices: 2.07 us -> 3.09 us  [per_device(): backs.append(lax.ppermute(back, AXES, home + list(zip(idle, alone))))]
    ppermute x4, starting transfers between devices: 3.68 us -> 3.11 us  [swap(): return lax.ppermute(x, AXES, [(d, d ^ k) for d in range(total)])]
    pallas_call x2 -> x3, Pallas kernels: 3.41 us -> 3.82 us  [visit(): pl.pallas_call(functools.partial(visit_kernel, ids, n + r, len(held), len...]
  transfers between devices with their start and end apart: 8 -> 8, of which waited for: 5 -> 4; matrix products, arithmetic and copies ran while one was open for 0% -> 0% of each run, Pallas kernels for 9% -> 11%
where the time goes in v4:
time: 34.1 us; the launch traced here: 33.9 us
  starting transfers between devices  11.6 us (34%)
  waiting for transfers between devices  10.8 us (32%)
  Pallas kernels  7.5 us (22%)
  blocking collectives  2.36 us (7%)
  local copies, waits for them, and re-layouts  1 us (3%)
  other arithmetic  0.59 us (2%)
    ppermute x2, waiting for transfers between devices, per_device(): visitors = [lax.ppermute(own, AXES, move) for move in moves]  7.99 us
    ppermute x2, starting transfers between devices, per_device(): visitors = [lax.ppermute(own, AXES, move) for move in moves]  5.37 us
    pallas_call x3, Pallas kernels, visit(): pl.pallas_call(functools.partial(visit_kernel, ids, n + r, len(held), len...  3.82 us
    ppermute x4, starting transfers between devices, swap(): return lax.ppermute(x, AXES, [(d, d ^ k) for d in range(total)])  3.11 us
    ppermute x2, starting transfers between devices, per_device(): backs.append(lax.ppermute(back, AXES, home + list(zip(idle, alone))))  3.09 us
    ppermute x4, waiting for transfers between devices, swap(): return lax.ppermute(x, AXES, [(d, d ^ k) for d in range(total)])  2.82 us
    all_gather x1, blocking collectives, per_device(): held.append(lax.all_gather(across, 'cols'))  2.36 us
    pallas_call x1, Pallas kernels, per_device(): pl.pallas_call(norm_kernel, out_shape=jax.ShapeDtypeStruct((rows, width),...  2.27 us
  transfers between devices with their start and end apart: 8, of which 4 were waited for; matrix products, arithmetic and copies ran while one was open for 0% of the time, Pallas kernels for 11%

profile of v4, /device:TPU:0, one launch (start us, length us, event | category | flops | bytes accessed | tf_op | source)
XLA Modules:
  0.0 33.9 jit_solution(1408204048128909896)
XLA Ops:
  0.0 0.0 copy-start.2
  0.0 0.0 copy-start.3
  0.0 0.0 copy-start.4
  0.0 2.3 %shard_map.55.refs_0_ = bf16[256,768]{1,0:T(8,128)(2,1)} custom-call(s32[4]{0:T(128)} %size_ref.7, s32[4]{0:T(128)} %start_ref.7, s32[1,256]{1,0:T(1,128)} %bitcast.6, f32[256,768]{1,0:T(8,128)} %emb_hbm.1), custom_call_target="tpu_custom_call" | custom-call | tf_op jit(solution)/shard_map/pallas_call | solution.py:150
  2.3 4.1 %collective-permute-start.3 = (bf16[256,768]{1,0:T(8,128)(2,1)}, bf16[256,768]{1,0:T(8,128)(2,1)S(1)}, u32[]{:S(2)}, u32[]{:S(2)}) collective-permute-start(bf16[256,768]{1,0:T(8,128)(2,1)} %shard_map.55.refs_0_), channel_id=1, source_target_pairs={{0,8},{1,9},{2,10},{3,11},{4,0},{5,1},{6,2},{7,3},{8,12},{9,13},{1... | collective-permute-start | bytes 1179656 | tf_op jit(solution)/shard_map/ppermute | solution.py:168
  6.4 0.0 collective-permute-start.1
  6.4 1.5 %collective-permute-start.2 = (bf16[256,768]{1,0:T(8,128)(2,1)}, bf16[256,768]{1,0:T(8,128)(2,1)S(1)}, u32[]{:S(2)}, u32[]{:S(2)}) collective-permute-start(bf16[256,768]{1,0:T(8,128)(2,1)} %shard_map.55.refs_0_), channel_id=1, source_target_pairs={{0,2},{1,3},{2,0},{3,1},{4,6},{5,7},{6,4},{7,5},{8,10},{9,11},{10,... | collective-permute-start | bytes 1179656 | tf_op jit(solution)/shard_map/ppermute | solution.py:166
  7.9 1.3 %collective-permute-start = (bf16[256,768]{1,0:T(8,128)(2,1)}, bf16[256,768]{1,0:T(8,128)(2,1)S(1)}, u32[]{:S(2)}, u32[]{:S(2)}) collective-permute-start(bf16[256,768]{1,0:T(8,128)(2,1)} %shard_map.55.refs_0_), channel_id=1, source_target_pairs={{4,8},{5,9},{6,10},{7,11},{12,0},{13,1},{14,2},{15,3},{20,24},{21,... | collective-permute-start | bytes 1179656 | tf_op jit(solution)/shard_map/ppermute | solution.py:168
  9.2 5.9 %collective-permute-done.3.visitor = bf16[256,768]{1,0:T(8,128)(2,1)S(1)} collective-permute-done((bf16[256,768]{1,0:T(8,128)(2,1)}, bf16[256,768]{1,0:T(8,128)(2,1)S(1)}, u32[]{:S(2)}, u32[]{:S(2)}) %collective-permute-start.3) | collective-permute-done | bytes 393248 | tf_op jit(solution)/shard_map/ppermute | solution.py:168
  15.1 0.0 collective-permute-done.1.refs_1_
  15.1 0.0 copy-done.2
  15.1 0.0 copy-done.3
  15.1 0.0 copy-done.4
  15.1 0.0 copy-start
  15.1 1.0 %copy-done = bf16[256,768]{1,0:T(8,128)(2,1)S(1)} copy-done((bf16[256,768]{1,0:T(8,128)(2,1)S(1)}, bf16[256,768]{1,0:T(8,128)(2,1)}, u32[]{:S(2)}) %copy-start) | copy-done | bytes 393240
  16.1 1.2 %shard_map.56 = (f32[1,256]{1,0:T(1,128)S(1)}, f32[1,256]{1,0:T(1,128)S(1)}, f32[1,256]{1,0:T(1,128)S(1)}) custom-call(s32[16,6]{1,0:T(8,128)S(1)} %copy-done.2, s32[4]{0:T(128)S(1)} %copy-done.3, s32[4]{0:T(128)S(1)} %copy-done.4, bf16[256,768]{1,0:T(8,128)(2,1)S(1)} %collective-permute-done.3.visitor, bf16[256,768]{1,0:T(8,128)(2,1)S(1)} %copy-done, ...), custom_call_target="tpu_custom_call" | custom-call | flops 201326592 | bytes 1179648 | tf_op jit(solution)/shard_map/pallas_call | solution.py:170
  17.3 0.8 %collective-permute-done.2 = bf16[256,768]{1,0:T(8,128)(2,1)S(1)} collective-permute-done((bf16[256,768]{1,0:T(8,128)(2,1)}, bf16[256,768]{1,0:T(8,128)(2,1)S(1)}, u32[]{:S(2)}, u32[]{:S(2)}) %collective-permute-start.2) | collective-permute-done | bytes 393248 | tf_op jit(solution)/shard_map/ppermute | solution.py:166
  18.1 2.4 %all-gather = bf16[512,768]{1,0:T(8,128)(2,1)S(1)} all-gather(bf16[256,768]{1,0:T(8,128)(2,1)S(1)} %collective-permute-done.2), channel_id=2, replica_groups=mesh['groups'=2,'rows'=8,'cols'=2] {'cols'}, dimensions={0}, use_global_device_ids=true | all-gather | bytes 1179648 | tf_op jit(solution)/shard_map/all_gather | solution.py:184
  20.5 1.2 %shard_map.58 = (f32[1,256]{1,0:T(1,128)S(1)}, f32[1,256]{1,0:T(1,128)S(1)}, f32[1,256]{1,0:T(1,128)S(1)}) custom-call(s32[16,6]{1,0:T(8,128)S(1)} %copy-done.2, s32[4]{0:T(128)S(1)} %copy-done.3, s32[4]{0:T(128)S(1)} %copy-done.4, bf16[256,768]{1,0:T(8,128)(2,1)S(1)} %collective-permute-done.3.visitor, bf16[2,256,768]{2,1,0:T(8,128)(2,1)S(1)} %bitcast.3), custom_call_target="tpu_custom_call" | custom-call | flops 201326592 | bytes 1179648 | tf_op jit(solution)/shard_map/pallas_call | solution.py:170
  21.7 0.0 copy-done.1
  21.7 1.4 %shard_map.57.refs_3_ = f32[1,256]{1,0:T(1,128)S(1)} custom-call(s32[16,6]{1,0:T(8,128)S(1)} %copy-done.2, s32[4]{0:T(128)S(1)} %copy-done.3, s32[4]{0:T(128)S(1)} %copy-done.4, f32[1,256]{1,0:T(1,128)S(1)} %get-tuple-element.22.before_ref, bf16[256,768]{1,0:T(8,128)(2,1)S(1)} %copy-done.1, bf16[256,768]{1,0:T(8,128)(2,1)S(1)} %collective-permute-done.1.refs_1_, ...), custom_call_target="tpu_custom_call" | custom-call | flops 402653184 | bytes 1572864 | tf_op jit(solution)/shard_map/pallas_call | solution.py:188
  23.1 2.1 %collective-permute-done.visitor = bf16[256,768]{1,0:T(8,128)(2,1)S(1)} collective-permute-done((bf16[256,768]{1,0:T(8,128)(2,1)}, bf16[256,768]{1,0:T(8,128)(2,1)S(1)}, u32[]{:S(2)}, u32[]{:S(2)}) %collective-permute-start) | collective-permute-done | bytes 393248 | tf_op jit(solution)/shard_map/ppermute | solution.py:168
  25.2 1.4 %shard_map.59 = (f32[1,256]{1,0:T(1,128)S(1)}, f32[1,256]{1,0:T(1,128)S(1)}, f32[1,256]{1,0:T(1,128)S(1)}, f32[1,256]{1,0:T(1,128)S(1)}, f32[1,256]{1,0:T(1,128)S(1)}) custom-call(s32[16,6]{1,0:T(8,128)S(1)} %copy-done.2, s32[4]{0:T(128)S(1)} %copy-done.3, s32[4]{0:T(128)S(1)} %copy-done.4, bf16[256,768]{1,0:T(8,128)(2,1)S(1)} %collective-permute-done.visitor, ...), custom_call_target="tpu_custom_call" | custom-call | flops 402653184 | bytes 1966080 | tf_op jit(solution)/shard_map/pallas_call | solution.py:170
  26.6 0.1 collective-permute-start.4
  26.7 0.7 %collective-permute-start.5 = (f32[1,256]{1,0:T(1,128)S(1)}, f32[1,256]{1,0:T(1,128)S(1)}, u32[]{:S(2)}, u32[]{:S(2)}) collective-permute-start(f32[1,256]{1,0:T(1,128)S(1)} %max.19), channel_id=1, source_target_pairs={{8,0},{9,1},{10,2},{11,3},{0,4},{1,5},{2,6},{3,7},{12,8},{13,9},{1... | collective-permute-start | bytes 3080 | tf_op jit(solution)/shard_map/ppermute | solution.py:203
  27.4 2.4 %collective-permute-start.6 = (f32[1,256]{1,0:T(1,128)S(1)}, f32[1,256]{1,0:T(1,128)S(1)}, u32[]{:S(2)}, u32[]{:S(2)}) collective-permute-start(f32[1,256]{1,0:T(1,128)S(1)} %get-tuple-element.31), channel_id=1, source_target_pairs={{8,4},{9,5},{10,6},{11,7},{0,12},{1,13},{2,14},{3,15},{4,0},{5,1},... | collective-permute-start | bytes 3080 | tf_op jit(solution)/shard_map/ppermute | solution.py:203
  29.8 0.0 collective-permute-done.4
  29.8 1.5 %collective-permute-start.7 = (f32[1,256]{1,0:T(1,128)S(1)}, f32[1,256]{1,0:T(1,128)S(1)}, u32[]{:S(2)}, u32[]{:S(2)}) collective-permute-start(f32[1,256]{1,0:T(1,128)S(1)} %slice_maximum_fusion), channel_id=1, source_target_pairs={{0,2},{1,3},{2,0},{3,1},{4,6},{5,7},{6,4},{7,5},{8,10},{9,11},{10,... | collective-permute-start | bytes 3080 | tf_op jit(solution)/shard_map/ppermute | solution.py:166
  31.3 0.0 collective-permute-done.5
  31.3 0.0 collective-permute-done.6
  31.3 2.0 %collective-permute-done.7 = f32[1,256]{1,0:T(1,128)S(1)} collective-permute-done((f32[1,256]{1,0:T(1,128)S(1)}, f32[1,256]{1,0:T(1,128)S(1)}, u32[]{:S(2)}, u32[]{:S(2)}) %collective-permute-start.7) | collective-permute-done | bytes 1056 | tf_op jit(solution)/shard_map/ppermute | solution.py:166
  33.4 0.6 %compare_select_fusion = f32[1,256]{1,0:T(1,128)} fusion(f32[1,256]{1,0:T(1,128)S(1)} %collective-permute-done.7, f32[1,256]{1,0:T(1,128)S(1)} %collective-permute-done.6, f32[1,256]{1,0:T(1,128)S(1)} %collective-permute-done.5, f32[1,256]{1,0:T(1,128)S(1)} %get-tuple-element.26, f32[2,256]{1,0:T(2,128)S(1)} %collective-permute-done.4), kind=kLoop, calls=%fused_computation | loop fusion | flops 1536 | bytes 6144 | tf_op jit(solution)/shard_map/jit(_where)/select_n | solution.py:214
  (4 shorter events, 0.0 us)
Async XLA Ops:
  0.0 15.1 %copy-start.2 = (s32[16,6]{1,0:T(8,128)S(1)}, s32[16,6]{1,0:T(8,128)}, u32[]{:S(2)}) copy-start(s32[16,6]{1,0:T(8,128)} %constant.6.clone.table_ref) | copy-start | bytes 1156
  0.0 15.1 %copy-start.3 = (s32[4]{0:T(128)S(1)}, s32[4]{0:T(128)}, u32[]{:S(2)}) copy-start(s32[4]{0:T(128)} %size_ref.7) | copy-start | bytes 52
  0.0 15.1 %copy-start.4 = (s32[4]{0:T(128)S(1)}, s32[4]{0:T(128)}, u32[]{:S(2)}) copy-start(s32[4]{0:T(128)} %start_ref.7) | copy-start | bytes 52
  2.3 12.8 %collective-permute-start.3 = (bf16[256,768]{1,0:T(8,128)(2,1)}, bf16[256,768]{1,0:T(8,128)(2,1)S(1)}, u32[]{:S(2)}, u32[]{:S(2)}) collective-permute-start(bf16[256,768]{1,0:T(8,128)(2,1)} %shard_map.55.refs_0_), channel_id=1, source_target_pairs={{0,8},{1,9},{2,10},{3,11},{4,0},{5,1},{6,2},{7,3},{8,12},{9,13},{1... | collective-permute-start | bytes 1179656 | tf_op jit(solution)/shard_map/ppermute | solution.py:168
  6.4 8.7 %collective-permute-start.1 = (bf16[256,768]{1,0:T(8,128)(2,1)}, bf16[256,768]{1,0:T(8,128)(2,1)S(1)}, u32[]{:S(2)}, u32[]{:S(2)}) collective-permute-start(bf16[256,768]{1,0:T(8,128)(2,1)} %shard_map.55.refs_0_), channel_id=1, source_target_pairs={{0,1},{1,0},{2,3},{3,2},{4,5},{5,4},{6,7},{7,6},{8,9},{9,8},{10,11... | collective-permute-start | bytes 1179656 | tf_op jit(solution)/shard_map/ppermute | solution.py:166
  6.4 11.7 %collective-permute-start.2 = (bf16[256,768]{1,0:T(8,128)(2,1)}, bf16[256,768]{1,0:T(8,128)(2,1)S(1)}, u32[]{:S(2)}, u32[]{:S(2)}) collective-permute-start(bf16[256,768]{1,0:T(8,128)(2,1)} %shard_map.55.refs_0_), channel_id=1, source_target_pairs={{0,2},{1,3},{2,0},{3,1},{4,6},{5,7},{6,4},{7,5},{8,10},{9,11},{10,... | collective-permute-start | bytes 1179656 | tf_op jit(solution)/shard_map/ppermute | solution.py:166
  7.9 17.3 %collective-permute-start = (bf16[256,768]{1,0:T(8,128)(2,1)}, bf16[256,768]{1,0:T(8,128)(2,1)S(1)}, u32[]{:S(2)}, u32[]{:S(2)}) collective-permute-start(bf16[256,768]{1,0:T(8,128)(2,1)} %shard_map.55.refs_0_), channel_id=1, source_target_pairs={{4,8},{5,9},{6,10},{7,11},{12,0},{13,1},{14,2},{15,3},{20,24},{21,... | collective-permute-start | bytes 1179656 | tf_op jit(solution)/shard_map/ppermute | solution.py:168
  15.1 1.0 %copy-start = (bf16[256,768]{1,0:T(8,128)(2,1)S(1)}, bf16[256,768]{1,0:T(8,128)(2,1)}, u32[]{:S(2)}) copy-start(bf16[256,768]{1,0:T(8,128)(2,1)} %shard_map.55.refs_0_) | copy-start | bytes 1179652
  20.5 1.2 %copy-start.1 = (bf16[256,768]{1,0:T(8,128)(2,1)S(1)}, bf16[256,768]{1,0:T(8,128)(2,1)}, u32[]{:S(2)}) copy-start(bf16[256,768]{1,0:T(8,128)(2,1)} %shard_map.55.refs_0_) | copy-start | bytes 1179652
  26.6 3.2 %collective-permute-start.4 = (f32[2,256]{1,0:T(2,128)S(1)}, f32[2,256]{1,0:T(2,128)S(1)}, u32[]{:S(2)}, u32[]{:S(2)}) collective-permute-start(f32[2,256]{1,0:T(2,128)S(1)} %pad_maximum_fusion), channel_id=1, source_target_pairs={{0,1},{1,0},{2,3},{3,2},{4,5},{5,4},{6,7},{7,6},{8,9},{9,8},{10,11... | collective-permute-start | bytes 6152 | tf_op jit(solution)/shard_map/ppermute | solution.py:166
  26.7 4.6 %collective-permute-start.5 = (f32[1,256]{1,0:T(1,128)S(1)}, f32[1,256]{1,0:T(1,128)S(1)}, u32[]{:S(2)}, u32[]{:S(2)}) collective-permute-start(f32[1,256]{1,0:T(1,128)S(1)} %max.19), channel_id=1, source_target_pairs={{8,0},{9,1},{10,2},{11,3},{0,4},{1,5},{2,6},{3,7},{12,8},{13,9},{1... | collective-permute-start | bytes 3080 | tf_op jit(solution)/shard_map/ppermute | solution.py:203
  27.4 3.9 %collective-permute-start.6 = (f32[1,256]{1,0:T(1,128)S(1)}, f32[1,256]{1,0:T(1,128)S(1)}, u32[]{:S(2)}, u32[]{:S(2)}) collective-permute-start(f32[1,256]{1,0:T(1,128)S(1)} %get-tuple-element.31), channel_id=1, source_target_pairs={{8,4},{9,5},{10,6},{11,7},{0,12},{1,13},{2,14},{3,15},{4,0},{5,1},... | collective-permute-start | bytes 3080 | tf_op jit(solution)/shard_map/ppermute | solution.py:203
  29.8 3.6 %collective-permute-start.7 = (f32[1,256]{1,0:T(1,128)S(1)}, f32[1,256]{1,0:T(1,128)S(1)}, u32[]{:S(2)}, u32[]{:S(2)}) collective-permute-start(f32[1,256]{1,0:T(1,128)S(1)} %slice_maximum_fusion), channel_id=1, source_target_pairs={{0,2},{1,3},{2,0},{3,1},{4,6},{5,7},{6,4},{7,5},{8,10},{9,11},{10,... | collective-permute-start | bytes 3080 | tf_op jit(solution)/shard_map/ppermute | solution.py:166

commit v5 on v4

--- a/solution.py
+++ b/solution.py
@@ -79,47 +79,36 @@
 
 
 def blocks_of(refs):
-    blocks = []
-    for ref in refs:
-        if len(ref.shape) == 2:
-            blocks.append(ref)
-        else:
-            blocks += [ref.at[lax.axis_index("cols") ^ k] for k in range(2)]
-    return blocks
-
-
-def column_kernel(table_ref, size_ref, start_ref, before_ref, *refs):
-    held, out_ref = blocks_of(refs[:-1]), refs[-1]
-    n = len(held)
-    rows = held[0].shape[0]
+    return [ref.at[lax.axis_index("cols") ^ k] for ref in refs for k in range(2)]
+
+
+def meet_kernel(ids, lefts, blocks, tops_before, rows_before, table_ref, size_ref, start_ref, *refs):
+    left_refs, refs = refs[: len(lefts)], refs[len(lefts) :]
+    left_refs = [blocks_of([ref])[0] if len(ref.shape) == 3 else ref for ref in left_refs]
+    held, refs = blocks_of(refs[:blocks]), refs[blocks:]
+    befores, outs = refs[: tops_before + rows_before], refs[tops_before + rows_before :]
+    rows = left_refs[0].shape[0]
     me = my_block()
-    own = held[0][...]
-    mine = row_labels(me, rows, size_ref, start_ref)
-    off = lax.broadcasted_iota(jnp.int32, (rows, rows), 0) != lax.broadcasted_iota(
-        jnp.int32, (rows, rows), 1
-    )
-    best = jnp.full((rows, 128), EMPTY, jnp.float32)
-    for k in range(n):
-        keys = labels(lanes(table_ref[me, k], rows), size_ref, start_ref)
-        best = jnp.maximum(best, fold(products(own, mine, held[k][...], keys, off if k == 0 else None)))
-    out_ref[...] = jnp.maximum(before_ref[...], jnp.max(best.T, axis=0, keepdims=True))
-
-
-def visit_kernel(ids, slot, blocks, befores, table_ref, size_ref, start_ref, visitor, *refs):
-    n = len(ids)
-    held, refs = blocks_of(refs[:blocks]), refs[blocks:]
-    before, (*outs, back_ref) = refs[:befores], refs[befores:]
-    rows = visitor.shape[0]
-    me = my_block()
-    theirs = row_labels(table_ref[me, slot], rows, size_ref, start_ref)
-    best = jnp.full((rows, 128), EMPTY, jnp.float32)
-    for k in range(n):
-        keys = labels(lanes(table_ref[me, ids[k]], rows), size_ref, start_ref)
-        sim = products(visitor[...], theirs, held[k][...], keys)
-        best = jnp.maximum(best, fold(sim))
-        top = jnp.max(sim, axis=0, keepdims=True)
-        outs[k][...] = jnp.maximum(top, before[k][...]) if befores else top
-    back_ref[...] = jnp.max(best.T, axis=0, keepdims=True)
+    keys = [labels(lanes(table_ref[me, k], rows), size_ref, start_ref) for k in ids]
+    tops = len(ids) if lefts[0] else 0
+    for n, (slot, left) in enumerate(zip(lefts, left_refs)):
+        mine = row_labels(table_ref[me, slot], rows, size_ref, start_ref)
+        best = jnp.full((rows, 128), EMPTY, jnp.float32)
+        for k, (block, key) in enumerate(zip(held, keys)):
+            off = None
+            if slot == ids[k]:
+                off = lax.broadcasted_iota(jnp.int32, (rows, rows), 0) != lax.broadcasted_iota(
+                    jnp.int32, (rows, rows), 1
+                )
+            sim = products(left[...], mine, block[...], key, off)
+            best = jnp.maximum(best, fold(sim))
+            if n == 0 and tops:
+                top = jnp.max(sim, axis=0, keepdims=True)
+                outs[k][...] = jnp.maximum(top, befores[k][...]) if k < tops_before else top
+        best = jnp.max(best.T, axis=0, keepdims=True)
+        if rows_before:
+            best = jnp.maximum(best, befores[tops_before + n][...])
+        outs[tops + n][...] = best
 
 
 def per_device(chips, embeddings, cluster_size, cluster_start, live):
@@ -166,41 +155,40 @@
         return lax.ppermute(x, AXES, [(d, d ^ k) for d in range(total)])
 
     visitors = [lax.ppermute(own, AXES, move) for move in moves]
-    def visit(r, ids, held, before):
-        *peaks, back = pl.pallas_call(
-            functools.partial(visit_kernel, ids, n + r, len(held), len(before)),
-            out_shape=[small] * (len(ids) + 1),
-            in_specs=[SMEM] * 3 + [VMEM] * (1 + len(held) + len(before)),
-            out_specs=[VMEM] * (len(ids) + 1),
+    def meet(ids, lefts, held, tops=(), rows_=()):
+        slots, blocks = zip(*lefts)
+        args = [*blocks, *held, *tops, *rows_]
+        outs = (len(ids) if slots[0] else 0) + len(lefts)
+        got = pl.pallas_call(
+            functools.partial(meet_kernel, ids, slots, len(held), len(tops), len(rows_)),
+            out_shape=[small] * outs,
+            in_specs=[SMEM] * 3 + [VMEM] * len(args),
+            out_specs=[VMEM] * outs,
             compiler_params=params,
-            cost_estimate=cost(len(ids), len(ids) + 1),
-        )(table, cluster_size, cluster_start, visitors[r], *held, *before)
-        return peaks, back
-
-    held = [own, swap(own, 1)]
-    peaks, back = visit(0, (0, 1), held, [])
+            cost_estimate=cost(len(ids) * len(lefts), len(ids) + len(lefts)),
+        )(table, cluster_size, cluster_start, *args)
+        return got[: outs - len(lefts)], got[outs - len(lefts) :]
+
+    held = [lax.all_gather(own, "cols")]
+    _, mine = meet((0, 1), [(0, held[0])], held)
+    peaks, (back,) = meet((0, 1), [(n, visitors[0])], held, mine)
     if tall == 2:
         across, *peaks = lax.optimization_barrier((swap(own, 2), *peaks))
         held.append(lax.all_gather(across, "cols"))
-        more, rest = visit(0, (2, 3), held[2:], [])
-        peaks, back = peaks + more, jnp.maximum(back, rest)
-
-    peaks[0] = pl.pallas_call(
-        column_kernel,
-        out_shape=small,
-        in_specs=[SMEM] * 3 + [VMEM] * (1 + len(held)),
-        out_specs=VMEM,
-        compiler_params=params,
-        cost_estimate=cost(n, n),
-    )(table, cluster_size, cluster_start, peaks[0], *held)
+        more, (back, mine) = meet((2, 3), [(n, visitors[0]), (0, held[0])], held[1:], (), (back, peaks[0]))
+        peaks = [mine, *peaks[1:], *more]
+
     backs = []
     for r, move in enumerate(moves):
         if r:
-            peaks, back = visit(r, tuple(range(n)), held, peaks)
+            peaks, (back,) = meet(tuple(range(n)), [(n + r, visitors[r])], held, peaks)
         home = [(t, s) for s, t in move]
         idle = sorted(set(range(total)) - {t for t, _ in home})
         alone = sorted(set(range(total)) - {s for _, s in home})
-        backs.append(lax.ppermute(back, AXES, home + list(zip(idle, alone))))
+        back = lax.ppermute(back, AXES, home + list(zip(idle, alone)))
+        if False:
+            back, peaks = lax.optimization_barrier((back, peaks))
+        backs.append(back)
 
     peak = peaks[0]
     if tall == 2:

time: 34.1 us -> 33.1 us (0.971)
  blocking collectives: 2.36 us -> 4.94 us
  waiting for transfers between devices: 10.8 us -> 8.58 us
  starting transfers between devices: 11.6 us -> 10.6 us
    all_gather x0 -> x1, blocking collectives: none -> 2.58 us  [per_device(): held = [lax.all_gather(own, 'cols')]]
    ppermute x2, waiting for transfers between devices: 7.99 us -> 5.7 us  [per_device(): visitors = [lax.ppermute(own, AXES, move) for move in moves]]
    ppermute x2, starting transfers between devices: 3.09 us -> 2.07 us  [per_device(): back = lax.ppermute(back, AXES, home + list(zip(idle, alone)))]
    ppermute x2, waiting for transfers between devices: 0.01 us -> 1 us  [per_device(): back = lax.ppermute(back, AXES, home + list(zip(idle, alone)))]
    ppermute x4 -> x3, waiting for transfers between devices: 2.82 us -> 1.88 us  [swap(): return lax.ppermute(x, AXES, [(d, d ^ k) for d in range(total)])]
    unnamed x10 -> x6, local copies, waits for them, and re-layouts: 1 us -> 0.67 us
    ppermute x4 -> x3, starting transfers between devices: 3.11 us -> 3.11 us  [swap(): return lax.ppermute(x, AXES, [(d, d ^ k) for d in range(total)])]
  transfers between devices with their start and end apart: 8 -> 7, of which waited for: 4 -> 5; matrix products, arithmetic and copies ran while one was open for 0% -> 0% of each run, Pallas kernels for 11% -> 12%
where the time goes in v5:
time: 33.1 us; the launch traced here: 32.9 us
  starting transfers between devices  10.6 us (32%)
  waiting for transfers between devices  8.58 us (26%)
  Pallas kernels  7.47 us (23%)
  blocking collectives  4.94 us (15%)
  local copies, waits for them, and re-layouts  0.67 us (2%)
  other arithmetic  0.58 us (2%)
    ppermute x2, waiting for transfers between devices, per_device(): visitors = [lax.ppermute(own, AXES, move) for move in moves]  5.7 us
    ppermute x2, starting transfers between devices, per_device(): visitors = [lax.ppermute(own, AXES, move) for move in moves]  5.37 us
    pallas_call x4, Pallas kernels, meet(): pl.pallas_call(functools.partial(meet_kernel, ids, slots, len(held), len(...  5.25 us
    ppermute x3, starting transfers between devices, swap(): return lax.ppermute(x, AXES, [(d, d ^ k) for d in range(total)])  3.11 us
    all_gather x1, blocking collectives, per_device(): held = [lax.all_gather(own, 'cols')]  2.58 us
    all_gather x1, blocking collectives, per_device(): held.append(lax.all_gather(across, 'cols'))  2.36 us
    pallas_call x1, Pallas kernels, per_device(): pl.pallas_call(norm_kernel, out_shape=jax.ShapeDtypeStruct((rows, width),...  2.22 us
    ppermute x2, starting transfers between devices, per_device(): back = lax.ppermute(back, AXES, home + list(zip(idle, alone)))  2.07 us
  transfers between devices with their start and end apart: 7, of which 5 were waited for; matrix products, arithmetic and copies ran while one was open for 0% of the time, Pallas kernels for 12%

profile of v5, /device:TPU:0, one launch (start us, length us, event | category | flops | bytes accessed | tf_op | source)
XLA Modules:
  0.0 32.9 jit_solution(1676979089363869586)
XLA Ops:
  0.0 2.2 %shard_map.55 = bf16[256,768]{1,0:T(8,128)(2,1)} custom-call(s32[4]{0:T(128)} %size_ref.7, s32[4]{0:T(128)} %start_ref.7, s32[1,256]{1,0:T(1,128)} %bitcast.11, f32[256,768]{1,0:T(8,128)} %emb_hbm.1), custom_call_target="tpu_custom_call" | custom-call | tf_op jit(solution)/shard_map/pallas_call | solution.py:139
  2.2 0.0 copy-start
  2.2 4.1 %collective-permute-start.2 = (bf16[256,768]{1,0:T(8,128)(2,1)}, bf16[256,768]{1,0:T(8,128)(2,1)S(1)}, u32[]{:S(2)}, u32[]{:S(2)}) collective-permute-start(bf16[256,768]{1,0:T(8,128)(2,1)} %shard_map.55), channel_id=1, source_target_pairs={{0,8},{1,9},{2,10},{3,11},{4,0},{5,1},{6,2},{7,3},{8,12},{9,13},{1... | collective-permute-start | bytes 1179656 | tf_op jit(solution)/shard_map/ppermute | solution.py:157
  6.3 1.5 %collective-permute-start.1 = (bf16[256,768]{1,0:T(8,128)(2,1)}, bf16[256,768]{1,0:T(8,128)(2,1)S(1)}, u32[]{:S(2)}, u32[]{:S(2)}) collective-permute-start(bf16[256,768]{1,0:T(8,128)(2,1)} %shard_map.55), channel_id=1, source_target_pairs={{0,2},{1,3},{2,0},{3,1},{4,6},{5,7},{6,4},{7,5},{8,10},{9,11},{10,... | collective-permute-start | bytes 1179656 | tf_op jit(solution)/shard_map/ppermute | solution.py:155
  7.9 1.3 %collective-permute-start = (bf16[256,768]{1,0:T(8,128)(2,1)}, bf16[256,768]{1,0:T(8,128)(2,1)S(1)}, u32[]{:S(2)}, u32[]{:S(2)}) collective-permute-start(bf16[256,768]{1,0:T(8,128)(2,1)} %shard_map.55), channel_id=1, source_target_pairs={{4,8},{5,9},{6,10},{7,11},{12,0},{13,1},{14,2},{15,3},{20,24},{21,... | collective-permute-start | bytes 1179656 | tf_op jit(solution)/shard_map/ppermute | solution.py:157
  9.1 2.6 %all-gather = bf16[512,768]{1,0:T(8,128)(2,1)S(1)} all-gather(bf16[256,768]{1,0:T(8,128)(2,1)} %shard_map.55), channel_id=2, replica_groups=mesh['groups'=2,'rows'=8,'cols'=2] {'cols'}, dimensions={0}, use_global_device_ids=true | all-gather | bytes 1179648 | tf_op jit(solution)/shard_map/all_gather | solution.py:172
  11.7 0.0 copy-start.1
  11.7 0.0 copy-start.2
  11.7 0.0 copy-done
  11.7 0.6 %copy-done.1 = s32[4]{0:T(128)S(1)} copy-done((s32[4]{0:T(128)S(1)}, s32[4]{0:T(128)}, u32[]{:S(2)}) %copy-start.1) | copy-done | bytes 40
  12.4 0.0 copy-done.2
  12.4 1.2 %shard_map.56.refs_2_ = f32[1,256]{1,0:T(1,128)S(1)} custom-call(s32[16,6]{1,0:T(8,128)S(1)} %copy-done, s32[4]{0:T(128)S(1)} %copy-done.1, s32[4]{0:T(128)S(1)} %copy-done.2, bf16[2,256,768]{2,1,0:T(8,128)(2,1)S(1)} %bitcast.4, bf16[2,256,768]{2,1,0:T(8,128)(2,1)S(1)} %bitcast.5), custom_call_target="tpu_custom_call" | custom-call | flops 201326592 | bytes 1179648 | tf_op jit(solution)/shard_map/pallas_call | solution.py:162
  13.6 1.4 %collective-permute-done.2.refs_0_ = bf16[256,768]{1,0:T(8,128)(2,1)S(1)} collective-permute-done((bf16[256,768]{1,0:T(8,128)(2,1)}, bf16[256,768]{1,0:T(8,128)(2,1)S(1)}, u32[]{:S(2)}, u32[]{:S(2)}) %collective-permute-start.2) | collective-permute-done | bytes 393248 | tf_op jit(solution)/shard_map/ppermute | solution.py:157
  15.1 1.2 %shard_map.57 = (f32[1,256]{1,0:T(1,128)S(1)}, f32[1,256]{1,0:T(1,128)S(1)}, f32[1,256]{1,0:T(1,128)S(1)}) custom-call(s32[16,6]{1,0:T(8,128)S(1)} %copy-done, s32[4]{0:T(128)S(1)} %copy-done.1, s32[4]{0:T(128)S(1)} %copy-done.2, bf16[256,768]{1,0:T(8,128)(2,1)S(1)} %collective-permute-done.2.refs_0_, bf16[2,256,768]{2,1,0:T(8,128)(2,1)S(1)} %bitcast.6, ...), custom_call_target="tpu_custom_call" | custom-call | flops 201326592 | bytes 1179648 | tf_op jit(solution)/shard_map/pallas_call | solution.py:162
  16.3 0.8 %collective-permute-done.1 = bf16[256,768]{1,0:T(8,128)(2,1)S(1)} collective-permute-done((bf16[256,768]{1,0:T(8,128)(2,1)}, bf16[256,768]{1,0:T(8,128)(2,1)S(1)}, u32[]{:S(2)}, u32[]{:S(2)}) %collective-permute-start.1) | collective-permute-done | bytes 393248 | tf_op jit(solution)/shard_map/ppermute | solution.py:155
  17.1 2.4 %all-gather.1 = bf16[512,768]{1,0:T(8,128)(2,1)S(1)} all-gather(bf16[256,768]{1,0:T(8,128)(2,1)S(1)} %collective-permute-done.1), channel_id=3, replica_groups=mesh['groups'=2,'rows'=8,'cols'=2] {'cols'}, dimensions={0}, use_global_device_ids=true | all-gather | bytes 1179648 | tf_op jit(solution)/shard_map/all_gather | solution.py:177
  19.5 1.4 %shard_map.58 = (f32[1,256]{1,0:T(1,128)S(1)}, f32[1,256]{1,0:T(1,128)S(1)}, f32[1,256]{1,0:T(1,128)S(1)}, f32[1,256]{1,0:T(1,128)S(1)}) custom-call(s32[16,6]{1,0:T(8,128)S(1)} %copy-done, s32[4]{0:T(128)S(1)} %copy-done.1, s32[4]{0:T(128)S(1)} %copy-done.2, bf16[256,768]{1,0:T(8,128)(2,1)S(1)} %collective-permute-done.2.refs_0_, ...), custom_call_target="tpu_custom_call" | custom-call | flops 402653184 | bytes 1572864 | tf_op jit(solution)/shard_map/pallas_call | solution.py:162
  20.9 4.2 %collective-permute-done.refs_0_ = bf16[256,768]{1,0:T(8,128)(2,1)S(1)} collective-permute-done((bf16[256,768]{1,0:T(8,128)(2,1)}, bf16[256,768]{1,0:T(8,128)(2,1)S(1)}, u32[]{:S(2)}, u32[]{:S(2)}) %collective-permute-start) | collective-permute-done | bytes 393248 | tf_op jit(solution)/shard_map/ppermute | solution.py:157
  25.1 1.4 %shard_map.59 = (f32[1,256]{1,0:T(1,128)S(1)}, f32[1,256]{1,0:T(1,128)S(1)}, f32[1,256]{1,0:T(1,128)S(1)}, f32[1,256]{1,0:T(1,128)S(1)}, f32[1,256]{1,0:T(1,128)S(1)}) custom-call(s32[16,6]{1,0:T(8,128)S(1)} %copy-done, s32[4]{0:T(128)S(1)} %copy-done.1, s32[4]{0:T(128)S(1)} %copy-done.2, bf16[256,768]{1,0:T(8,128)(2,1)S(1)} %collective-permute-done.refs_0_, ...), custom_call_target="tpu_custom_call" | custom-call | flops 402653184 | bytes 1966080 | tf_op jit(solution)/shard_map/pallas_call | solution.py:162
  26.6 0.1 collective-permute-start.3
  26.7 0.1 collective-permute-start.5
  26.7 2.0 %collective-permute-start.4 = (f32[1,256]{1,0:T(1,128)S(1)}, f32[1,256]{1,0:T(1,128)S(1)}, u32[]{:S(2)}, u32[]{:S(2)}) collective-permute-start(f32[1,256]{1,0:T(1,128)S(1)} %get-tuple-element.32), channel_id=1, source_target_pairs={{8,0},{9,1},{10,2},{11,3},{0,4},{1,5},{2,6},{3,7},{12,8},{13,9},{1... | collective-permute-start | bytes 3080 | tf_op jit(solution)/shard_map/ppermute | solution.py:188
  28.7 0.0 collective-permute-done.3
  28.7 1.5 %collective-permute-start.6 = (f32[1,256]{1,0:T(1,128)S(1)}, f32[1,256]{1,0:T(1,128)S(1)}, u32[]{:S(2)}, u32[]{:S(2)}) collective-permute-start(f32[1,256]{1,0:T(1,128)S(1)} %slice_maximum_fusion), channel_id=1, source_target_pairs={{0,2},{1,3},{2,0},{3,1},{4,6},{5,7},{6,4},{7,5},{8,10},{9,11},{10,... | collective-permute-start | bytes 3080 | tf_op jit(solution)/shard_map/ppermute | solution.py:155
  30.3 0.0 collective-permute-done.5
  30.3 1.0 %collective-permute-done.4 = f32[1,256]{1,0:T(1,128)S(1)} collective-permute-done((f32[1,256]{1,0:T(1,128)S(1)}, f32[1,256]{1,0:T(1,128)S(1)}, u32[]{:S(2)}, u32[]{:S(2)}) %collective-permute-start.4) | collective-permute-done | bytes 1056 | tf_op jit(solution)/shard_map/ppermute | solution.py:188
  31.3 1.1 %collective-permute-done.6 = f32[1,256]{1,0:T(1,128)S(1)} collective-permute-done((f32[1,256]{1,0:T(1,128)S(1)}, f32[1,256]{1,0:T(1,128)S(1)}, u32[]{:S(2)}, u32[]{:S(2)}) %collective-permute-start.6) | collective-permute-done | bytes 1056 | tf_op jit(solution)/shard_map/ppermute | solution.py:155
  32.3 0.6 %compare_select_fusion = f32[1,256]{1,0:T(1,128)} fusion(f32[1,256]{1,0:T(1,128)S(1)} %collective-permute-done.6, f32[1,256]{1,0:T(1,128)S(1)} %collective-permute-done.5, f32[1,256]{1,0:T(1,128)S(1)} %collective-permute-done.4, f32[1,256]{1,0:T(1,128)S(1)} %get-tuple-element.29, f32[2,256]{1,0:T(2,128)S(1)} %collective-permute-done.3), kind=kLoop, calls=%fused_computation | loop fusion | flops 1536 | bytes 6144 | tf_op jit(solution)/shard_map/jit(_where)/select_n | solution.py:202
  (2 shorter events, 0.0 us)
Async XLA Ops:
  2.2 9.5 %copy-start = (s32[16,6]{1,0:T(8,128)S(1)}, s32[16,6]{1,0:T(8,128)}, u32[]{:S(2)}) copy-start(s32[16,6]{1,0:T(8,128)} %constant.6.clone.table_ref) | copy-start | bytes 1156
  2.2 12.8 %collective-permute-start.2 = (bf16[256,768]{1,0:T(8,128)(2,1)}, bf16[256,768]{1,0:T(8,128)(2,1)S(1)}, u32[]{:S(2)}, u32[]{:S(2)}) collective-permute-start(bf16[256,768]{1,0:T(8,128)(2,1)} %shard_map.55), channel_id=1, source_target_pairs={{0,8},{1,9},{2,10},{3,11},{4,0},{5,1},{6,2},{7,3},{8,12},{9,13},{1... | collective-permute-start | bytes 1179656 | tf_op jit(solution)/shard_map/ppermute | solution.py:157
  6.3 10.8 %collective-permute-start.1 = (bf16[256,768]{1,0:T(8,128)(2,1)}, bf16[256,768]{1,0:T(8,128)(2,1)S(1)}, u32[]{:S(2)}, u32[]{:S(2)}) collective-permute-start(bf16[256,768]{1,0:T(8,128)(2,1)} %shard_map.55), channel_id=1, source_target_pairs={{0,2},{1,3},{2,0},{3,1},{4,6},{5,7},{6,4},{7,5},{8,10},{9,11},{10,... | collective-permute-start | bytes 1179656 | tf_op jit(solution)/shard_map/ppermute | solution.py:155
  7.9 17.3 %collective-permute-start = (bf16[256,768]{1,0:T(8,128)(2,1)}, bf16[256,768]{1,0:T(8,128)(2,1)S(1)}, u32[]{:S(2)}, u32[]{:S(2)}) collective-permute-start(bf16[256,768]{1,0:T(8,128)(2,1)} %shard_map.55), channel_id=1, source_target_pairs={{4,8},{5,9},{6,10},{7,11},{12,0},{13,1},{14,2},{15,3},{20,24},{21,... | collective-permute-start | bytes 1179656 | tf_op jit(solution)/shard_map/ppermute | solution.py:157
  11.7 0.7 %copy-start.1 = (s32[4]{0:T(128)S(1)}, s32[4]{0:T(128)}, u32[]{:S(2)}) copy-start(s32[4]{0:T(128)} %size_ref.7) | copy-start | bytes 52
  11.7 0.7 %copy-start.2 = (s32[4]{0:T(128)S(1)}, s32[4]{0:T(128)}, u32[]{:S(2)}) copy-start(s32[4]{0:T(128)} %start_ref.7) | copy-start | bytes 52
  26.6 2.2 %collective-permute-start.3 = (f32[2,256]{1,0:T(2,128)S(1)}, f32[2,256]{1,0:T(2,128)S(1)}, u32[]{:S(2)}, u32[]{:S(2)}) collective-permute-start(f32[2,256]{1,0:T(2,128)S(1)} %pad_maximum_fusion), channel_id=1, source_target_pairs={{0,1},{1,0},{2,3},{3,2},{4,5},{5,4},{6,7},{7,6},{8,9},{9,8},{10,11... | collective-permute-start | bytes 6152 | tf_op jit(solution)/shard_map/ppermute | solution.py:155
  26.7 3.6 %collective-permute-start.5 = (f32[1,256]{1,0:T(1,128)S(1)}, f32[1,256]{1,0:T(1,128)S(1)}, u32[]{:S(2)}, u32[]{:S(2)}) collective-permute-start(f32[1,256]{1,0:T(1,128)S(1)} %get-tuple-element.33), channel_id=1, source_target_pairs={{8,4},{9,5},{10,6},{11,7},{0,12},{1,13},{2,14},{3,15},{4,0},{5,1},... | collective-permute-start | bytes 3080 | tf_op jit(solution)/shard_map/ppermute | solution.py:188
  26.7 4.5 %collective-permute-start.4 = (f32[1,256]{1,0:T(1,128)S(1)}, f32[1,256]{1,0:T(1,128)S(1)}, u32[]{:S(2)}, u32[]{:S(2)}) collective-permute-start(f32[1,256]{1,0:T(1,128)S(1)} %get-tuple-element.32), channel_id=1, source_target_pairs={{8,0},{9,1},{10,2},{11,3},{0,4},{1,5},{2,6},{3,7},{12,8},{13,9},{1... | collective-permute-start | bytes 3080 | tf_op jit(solution)/shard_map/ppermute | solution.py:188
  28.7 3.6 %collective-permute-start.6 = (f32[1,256]{1,0:T(1,128)S(1)}, f32[1,256]{1,0:T(1,128)S(1)}, u32[]{:S(2)}, u32[]{:S(2)}) collective-permute-start(f32[1,256]{1,0:T(1,128)S(1)} %slice_maximum_fusion), channel_id=1, source_target_pairs={{0,2},{1,3},{2,0},{3,1},{4,6},{5,7},{6,4},{7,5},{8,10},{9,11},{10,... | collective-permute-start | bytes 3080 | tf_op jit(solution)/shard_map/ppermute | solution.py:155

commit v6 on v5

--- a/solution.py
+++ b/solution.py
@@ -185,10 +185,8 @@
         home = [(t, s) for s, t in move]
         idle = sorted(set(range(total)) - {t for t, _ in home})
         alone = sorted(set(range(total)) - {s for _, s in home})
-        back = lax.ppermute(back, AXES, home + list(zip(idle, alone)))
-        if False:
-            back, peaks = lax.optimization_barrier((back, peaks))
-        backs.append(back)
+        backs.append(lax.ppermute(back, AXES, home + list(zip(idle, alone))))
+    backs[0], peaks = lax.optimization_barrier((backs[0], peaks))
 
     peak = peaks[0]
     if tall == 2:

time: 33.1 us -> 32.3 us (0.976)
  waiting for transfers between devices: 8.58 us -> 5.98 us
  starting transfers between devices: 10.6 us -> 12.4 us
    ppermute x2, waiting for transfers between devices: 5.7 us -> 3.1 us  [per_device(): visitors = [lax.ppermute(own, AXES, move) for move in moves]]
    ppermute x2, starting transfers between devices: 2.07 us -> 3.96 us  [per_device(): backs.append(lax.ppermute(back, AXES, home + list(zip(idle, alone))))]
  transfers between devices with their start and end apart: 7 -> 7, of which waited for: 5 -> 5; matrix products, arithmetic and copies ran while one was open for 0% -> 0% of each run, Pallas kernels for 12% -> 16%
where the time goes in v6:
time: 32.3 us; the launch traced here: 32.2 us
  starting transfers between devices  12.4 us (38%)
  Pallas kernels  7.48 us (23%)
  waiting for transfers between devices  5.98 us (19%)
  blocking collectives  4.94 us (15%)
  local copies, waits for them, and re-layouts  0.67 us (2%)
  other arithmetic  0.58 us (2%)
    ppermute x2, starting transfers between devices, per_device(): visitors = [lax.ppermute(own, AXES, move) for move in moves]  5.37 us
    pallas_call x4, Pallas kernels, meet(): pl.pallas_call(functools.partial(meet_kernel, ids, slots, len(held), len(...  5.26 us
    ppermute x2, starting transfers between devices, per_device(): backs.append(lax.ppermute(back, AXES, home + list(zip(idle, alone))))  3.96 us
    ppermute x3, starting transfers between devices, swap(): return lax.ppermute(x, AXES, [(d, d ^ k) for d in range(total)])  3.11 us
    ppermute x2, waiting for transfers between devices, per_device(): visitors = [lax.ppermute(own, AXES, move) for move in moves]  3.1 us
    all_gather x1, blocking collectives, per_device(): held = [lax.all_gather(own, 'cols')]  2.58 us
    all_gather x1, blocking collectives, per_device(): held.append(lax.all_gather(across, 'cols'))  2.36 us
    pallas_call x1, Pallas kernels, per_device(): pl.pallas_call(norm_kernel, out_shape=jax.ShapeDtypeStruct((rows, width),...  2.22 us
  transfers between devices with their start and end apart: 7, of which 5 were waited for; matrix products, arithmetic and copies ran while one was open for 0% of the time, Pallas kernels for 16%

profile of v6, /device:TPU:0, one launch (start us, length us, event | category | flops | bytes accessed | tf_op | source)
XLA Modules:
  0.0 32.2 jit_solution(16315562857667070910)
XLA Ops:
  0.0 2.2 %shard_map.55 = bf16[256,768]{1,0:T(8,128)(2,1)} custom-call(s32[4]{0:T(128)} %size_ref.7, s32[4]{0:T(128)} %start_ref.7, s32[1,256]{1,0:T(1,128)} %bitcast.11, f32[256,768]{1,0:T(8,128)} %emb_hbm.1), custom_call_target="tpu_custom_call" | custom-call | tf_op jit(solution)/shard_map/pallas_call | solution.py:139
  2.2 0.0 copy-start
  2.2 4.1 %collective-permute-start = (bf16[256,768]{1,0:T(8,128)(2,1)}, bf16[256,768]{1,0:T(8,128)(2,1)S(1)}, u32[]{:S(2)}, u32[]{:S(2)}) collective-permute-start(bf16[256,768]{1,0:T(8,128)(2,1)} %shard_map.55), channel_id=1, source_target_pairs={{0,8},{1,9},{2,10},{3,11},{4,0},{5,1},{6,2},{7,3},{8,12},{9,13},{1... | collective-permute-start | bytes 1179656 | tf_op jit(solution)/shard_map/ppermute | solution.py:157
  6.3 1.5 %collective-permute-start.1 = (bf16[256,768]{1,0:T(8,128)(2,1)}, bf16[256,768]{1,0:T(8,128)(2,1)S(1)}, u32[]{:S(2)}, u32[]{:S(2)}) collective-permute-start(bf16[256,768]{1,0:T(8,128)(2,1)} %shard_map.55), channel_id=1, source_target_pairs={{0,2},{1,3},{2,0},{3,1},{4,6},{5,7},{6,4},{7,5},{8,10},{9,11},{10,... | collective-permute-start | bytes 1179656 | tf_op jit(solution)/shard_map/ppermute | solution.py:155
  7.9 1.3 %collective-permute-start.3 = (bf16[256,768]{1,0:T(8,128)(2,1)}, bf16[256,768]{1,0:T(8,128)(2,1)S(1)}, u32[]{:S(2)}, u32[]{:S(2)}) collective-permute-start(bf16[256,768]{1,0:T(8,128)(2,1)} %shard_map.55), channel_id=1, source_target_pairs={{4,8},{5,9},{6,10},{7,11},{12,0},{13,1},{14,2},{15,3},{20,24},{21,... | collective-permute-start | bytes 1179656 | tf_op jit(solution)/shard_map/ppermute | solution.py:157
  9.1 2.6 %all-gather = bf16[512,768]{1,0:T(8,128)(2,1)S(1)} all-gather(bf16[256,768]{1,0:T(8,128)(2,1)} %shard_map.55), channel_id=2, replica_groups=mesh['groups'=2,'rows'=8,'cols'=2] {'cols'}, dimensions={0}, use_global_device_ids=true | all-gather | bytes 1179648 | tf_op jit(solution)/shard_map/all_gather | solution.py:172
  11.7 0.0 copy-start.1
  11.7 0.0 copy-start.2
  11.7 0.0 copy-done
  11.7 0.6 %copy-done.1 = s32[4]{0:T(128)S(1)} copy-done((s32[4]{0:T(128)S(1)}, s32[4]{0:T(128)}, u32[]{:S(2)}) %copy-start.1) | copy-done | bytes 40
  12.4 0.0 copy-done.2
  12.4 1.2 %shard_map.56.refs_2_ = f32[1,256]{1,0:T(1,128)S(1)} custom-call(s32[16,6]{1,0:T(8,128)S(1)} %copy-done, s32[4]{0:T(128)S(1)} %copy-done.1, s32[4]{0:T(128)S(1)} %copy-done.2, bf16[2,256,768]{2,1,0:T(8,128)(2,1)S(1)} %bitcast.4, bf16[2,256,768]{2,1,0:T(8,128)(2,1)S(1)} %bitcast.5), custom_call_target="tpu_custom_call" | custom-call | flops 201326592 | bytes 1179648 | tf_op jit(solution)/shard_map/pallas_call | solution.py:162
  13.6 1.4 %collective-permute-done.refs_0_ = bf16[256,768]{1,0:T(8,128)(2,1)S(1)} collective-permute-done((bf16[256,768]{1,0:T(8,128)(2,1)}, bf16[256,768]{1,0:T(8,128)(2,1)S(1)}, u32[]{:S(2)}, u32[]{:S(2)}) %collective-permute-start) | collective-permute-done | bytes 393248 | tf_op jit(solution)/shard_map/ppermute | solution.py:157
  15.1 1.2 %shard_map.57 = (f32[1,256]{1,0:T(1,128)S(1)}, f32[1,256]{1,0:T(1,128)S(1)}, f32[1,256]{1,0:T(1,128)S(1)}) custom-call(s32[16,6]{1,0:T(8,128)S(1)} %copy-done, s32[4]{0:T(128)S(1)} %copy-done.1, s32[4]{0:T(128)S(1)} %copy-done.2, bf16[256,768]{1,0:T(8,128)(2,1)S(1)} %collective-permute-done.refs_0_, bf16[2,256,768]{2,1,0:T(8,128)(2,1)S(1)} %bitcast.6, ...), custom_call_target="tpu_custom_call" | custom-call | flops 201326592 | bytes 1179648 | tf_op jit(solution)/shard_map/pallas_call | solution.py:162
  16.3 0.8 %collective-permute-done.1 = bf16[256,768]{1,0:T(8,128)(2,1)S(1)} collective-permute-done((bf16[256,768]{1,0:T(8,128)(2,1)}, bf16[256,768]{1,0:T(8,128)(2,1)S(1)}, u32[]{:S(2)}, u32[]{:S(2)}) %collective-permute-start.1) | collective-permute-done | bytes 393248 | tf_op jit(solution)/shard_map/ppermute | solution.py:155
  17.1 2.4 %all-gather.1 = bf16[512,768]{1,0:T(8,128)(2,1)S(1)} all-gather(bf16[256,768]{1,0:T(8,128)(2,1)S(1)} %collective-permute-done.1), channel_id=3, replica_groups=mesh['groups'=2,'rows'=8,'cols'=2] {'cols'}, dimensions={0}, use_global_device_ids=true | all-gather | bytes 1179648 | tf_op jit(solution)/shard_map/all_gather | solution.py:177
  19.5 1.4 %shard_map.58 = (f32[1,256]{1,0:T(1,128)S(1)}, f32[1,256]{1,0:T(1,128)S(1)}, f32[1,256]{1,0:T(1,128)S(1)}, f32[1,256]{1,0:T(1,128)S(1)}) custom-call(s32[16,6]{1,0:T(8,128)S(1)} %copy-done, s32[4]{0:T(128)S(1)} %copy-done.1, s32[4]{0:T(128)S(1)} %copy-done.2, bf16[256,768]{1,0:T(8,128)(2,1)S(1)} %collective-permute-done.refs_0_, ...), custom_call_target="tpu_custom_call" | custom-call | flops 402653184 | bytes 1572864 | tf_op jit(solution)/shard_map/pallas_call | solution.py:162
  20.9 2.6 %collective-permute-start.2 = (f32[1,256]{1,0:T(1,128)S(1)}, f32[1,256]{1,0:T(1,128)S(1)}, u32[]{:S(2)}, u32[]{:S(2)}) collective-permute-start(f32[1,256]{1,0:T(1,128)S(1)} %get-tuple-element.30), channel_id=1, source_target_pairs={{8,0},{9,1},{10,2},{11,3},{0,4},{1,5},{2,6},{3,7},{12,8},{13,9},{1... | collective-permute-start | bytes 3080 | tf_op jit(solution)/shard_map/ppermute | solution.py:188
  23.5 1.6 %collective-permute-done.3.refs_0_ = bf16[256,768]{1,0:T(8,128)(2,1)S(1)} collective-permute-done((bf16[256,768]{1,0:T(8,128)(2,1)}, bf16[256,768]{1,0:T(8,128)(2,1)S(1)}, u32[]{:S(2)}, u32[]{:S(2)}) %collective-permute-start.3) | collective-permute-done | bytes 393248 | tf_op jit(solution)/shard_map/ppermute | solution.py:157
  25.2 1.4 %shard_map.59 = (f32[1,256]{1,0:T(1,128)S(1)}, f32[1,256]{1,0:T(1,128)S(1)}, f32[1,256]{1,0:T(1,128)S(1)}, f32[1,256]{1,0:T(1,128)S(1)}, f32[1,256]{1,0:T(1,128)S(1)}) custom-call(s32[16,6]{1,0:T(8,128)S(1)} %copy-done, s32[4]{0:T(128)S(1)} %copy-done.1, s32[4]{0:T(128)S(1)} %copy-done.2, bf16[256,768]{1,0:T(8,128)(2,1)S(1)} %collective-permute-done.3.refs_0_, ...), custom_call_target="tpu_custom_call" | custom-call | flops 402653184 | bytes 1966080 | tf_op jit(solution)/shard_map/pallas_call | solution.py:162
  26.6 0.0 collective-permute-done.2
  26.6 0.1 collective-permute-start.4
  26.7 1.3 %collective-permute-start.5 = (f32[1,256]{1,0:T(1,128)S(1)}, f32[1,256]{1,0:T(1,128)S(1)}, u32[]{:S(2)}, u32[]{:S(2)}) collective-permute-start(f32[1,256]{1,0:T(1,128)S(1)} %get-tuple-element.43), channel_id=1, source_target_pairs={{8,4},{9,5},{10,6},{11,7},{0,12},{1,13},{2,14},{3,15},{4,0},{5,1},... | collective-permute-start | bytes 3080 | tf_op jit(solution)/shard_map/ppermute | solution.py:188
  28.0 0.0 collective-permute-done.4
  28.0 1.5 %collective-permute-start.6 = (f32[1,256]{1,0:T(1,128)S(1)}, f32[1,256]{1,0:T(1,128)S(1)}, u32[]{:S(2)}, u32[]{:S(2)}) collective-permute-start(f32[1,256]{1,0:T(1,128)S(1)} %slice_maximum_fusion), channel_id=1, source_target_pairs={{0,2},{1,3},{2,0},{3,1},{4,6},{5,7},{6,4},{7,5},{8,10},{9,11},{10,... | collective-permute-start | bytes 3080 | tf_op jit(solution)/shard_map/ppermute | solution.py:155
  29.6 0.7 %collective-permute-done.5 = f32[1,256]{1,0:T(1,128)S(1)} collective-permute-done((f32[1,256]{1,0:T(1,128)S(1)}, f32[1,256]{1,0:T(1,128)S(1)}, u32[]{:S(2)}, u32[]{:S(2)}) %collective-permute-start.5) | collective-permute-done | bytes 1056 | tf_op jit(solution)/shard_map/ppermute | solution.py:188
  30.3 1.3 %collective-permute-done.6 = f32[1,256]{1,0:T(1,128)S(1)} collective-permute-done((f32[1,256]{1,0:T(1,128)S(1)}, f32[1,256]{1,0:T(1,128)S(1)}, u32[]{:S(2)}, u32[]{:S(2)}) %collective-permute-start.6) | collective-permute-done | bytes 1056 | tf_op jit(solution)/shard_map/ppermute | solution.py:155
  31.6 0.6 %compare_select_fusion = f32[1,256]{1,0:T(1,128)} fusion(f32[1,256]{1,0:T(1,128)S(1)} %collective-permute-done.6, f32[1,256]{1,0:T(1,128)S(1)} %collective-permute-done.5, f32[1,256]{1,0:T(1,128)S(1)} %collective-permute-done.2, f32[1,256]{1,0:T(1,128)S(1)} %get-tuple-element.39, f32[2,256]{1,0:T(2,128)S(1)} %collective-permute-done.4), kind=kLoop, calls=%fused_computation | loop fusion | flops 1536 | bytes 6144 | tf_op jit(solution)/shard_map/jit(_where)/select_n | solution.py:200
  (2 shorter events, 0.0 us)
Async XLA Ops:
  2.2 9.5 %copy-start = (s32[16,6]{1,0:T(8,128)S(1)}, s32[16,6]{1,0:T(8,128)}, u32[]{:S(2)}) copy-start(s32[16,6]{1,0:T(8,128)} %constant.6.clone.table_ref) | copy-start | bytes 1156
  2.2 12.8 %collective-permute-start = (bf16[256,768]{1,0:T(8,128)(2,1)}, bf16[256,768]{1,0:T(8,128)(2,1)S(1)}, u32[]{:S(2)}, u32[]{:S(2)}) collective-permute-start(bf16[256,768]{1,0:T(8,128)(2,1)} %shard_map.55), channel_id=1, source_target_pairs={{0,8},{1,9},{2,10},{3,11},{4,0},{5,1},{6,2},{7,3},{8,12},{9,13},{1... | collective-permute-start | bytes 1179656 | tf_op jit(solution)/shard_map/ppermute | solution.py:157
  6.3 10.8 %collective-permute-start.1 = (bf16[256,768]{1,0:T(8,128)(2,1)}, bf16[256,768]{1,0:T(8,128)(2,1)S(1)}, u32[]{:S(2)}, u32[]{:S(2)}) collective-permute-start(bf16[256,768]{1,0:T(8,128)(2,1)} %shard_map.55), channel_id=1, source_target_pairs={{0,2},{1,3},{2,0},{3,1},{4,6},{5,7},{6,4},{7,5},{8,10},{9,11},{10,... | collective-permute-start | bytes 1179656 | tf_op jit(solution)/shard_map/ppermute | solution.py:155
  7.9 17.3 %collective-permute-start.3 = (bf16[256,768]{1,0:T(8,128)(2,1)}, bf16[256,768]{1,0:T(8,128)(2,1)S(1)}, u32[]{:S(2)}, u32[]{:S(2)}) collective-permute-start(bf16[256,768]{1,0:T(8,128)(2,1)} %shard_map.55), channel_id=1, source_target_pairs={{4,8},{5,9},{6,10},{7,11},{12,0},{13,1},{14,2},{15,3},{20,24},{21,... | collective-permute-start | bytes 1179656 | tf_op jit(solution)/shard_map/ppermute | solution.py:157
  11.7 0.7 %copy-start.1 = (s32[4]{0:T(128)S(1)}, s32[4]{0:T(128)}, u32[]{:S(2)}) copy-start(s32[4]{0:T(128)} %size_ref.7) | copy-start | bytes 52
  11.7 0.7 %copy-start.2 = (s32[4]{0:T(128)S(1)}, s32[4]{0:T(128)}, u32[]{:S(2)}) copy-start(s32[4]{0:T(128)} %start_ref.7) | copy-start | bytes 52
  20.9 5.7 %collective-permute-start.2 = (f32[1,256]{1,0:T(1,128)S(1)}, f32[1,256]{1,0:T(1,128)S(1)}, u32[]{:S(2)}, u32[]{:S(2)}) collective-permute-start(f32[1,256]{1,0:T(1,128)S(1)} %get-tuple-element.30), channel_id=1, source_target_pairs={{8,0},{9,1},{10,2},{11,3},{0,4},{1,5},{2,6},{3,7},{12,8},{13,9},{1... | collective-permute-start | bytes 3080 | tf_op jit(solution)/shard_map/ppermute | solution.py:188
  26.6 1.4 %collective-permute-start.4 = (f32[2,256]{1,0:T(2,128)S(1)}, f32[2,256]{1,0:T(2,128)S(1)}, u32[]{:S(2)}, u32[]{:S(2)}) collective-permute-start(f32[2,256]{1,0:T(2,128)S(1)} %pad_maximum_fusion), channel_id=1, source_target_pairs={{0,1},{1,0},{2,3},{3,2},{4,5},{5,4},{6,7},{7,6},{8,9},{9,8},{10,11... | collective-permute-start | bytes 6152 | tf_op jit(solution)/shard_map/ppermute | solution.py:155
  26.7 3.6 %collective-permute-start.5 = (f32[1,256]{1,0:T(1,128)S(1)}, f32[1,256]{1,0:T(1,128)S(1)}, u32[]{:S(2)}, u32[]{:S(2)}) collective-permute-start(f32[1,256]{1,0:T(1,128)S(1)} %get-tuple-element.43), channel_id=1, source_target_pairs={{8,4},{9,5},{10,6},{11,7},{0,12},{1,13},{2,14},{3,15},{4,0},{5,1},... | collective-permute-start | bytes 3080 | tf_op jit(solution)/shard_map/ppermute | solution.py:188
  28.0 3.6 %collective-permute-start.6 = (f32[1,256]{1,0:T(1,128)S(1)}, f32[1,256]{1,0:T(1,128)S(1)}, u32[]{:S(2)}, u32[]{:S(2)}) collective-permute-start(f32[1,256]{1,0:T(1,128)S(1)} %slice_maximum_fusion), channel_id=1, source_target_pairs={{0,2},{1,3},{2,0},{3,1},{4,6},{5,7},{6,4},{7,5},{8,10},{9,11},{10,... | collective-permute-start | bytes 3080 | tf_op jit(solution)/shard_map/ppermute | solution.py:155

commit v7 on v6

--- a/solution.py
+++ b/solution.py
@@ -17,7 +17,7 @@
 
 def layout(chips):
     if chips == 8:
-        return 2, [[(0, 2), (1, 0), (2, 3), (3, 1)], [(1, 2), (3, 0)]]
+        return 2, [[(0, 2), (1, 0), (2, 3), (3, 1)], [(2, 1), (0, 3)]]
     rounds = [[(c, (c + d) % chips) for c in range(chips)] for d in range(1, (chips + 1) // 2)]
     if chips % 2 == 0:
         rounds.append([(c, c + chips // 2) for c in range(chips // 2)])
@@ -175,8 +175,8 @@
     if tall == 2:
         across, *peaks = lax.optimization_barrier((swap(own, 2), *peaks))
         held.append(lax.all_gather(across, "cols"))
-        more, (back, mine) = meet((2, 3), [(n, visitors[0]), (0, held[0])], held[1:], (), (back, peaks[0]))
-        peaks = [mine, *peaks[1:], *more]
+        more, (back,) = meet((2, 3), [(n, visitors[0])], held[1:], (), (back,))
+        peaks += more
 
     backs = []
     for r, move in enumerate(moves):
@@ -190,6 +190,8 @@
 
     peak = peaks[0]
     if tall == 2:
+        _, mine = meet((2, 3), [(0, held[0])], held[1:])
+        peak = jnp.maximum(peak, mine[0])
         other = swap(jnp.concatenate([peaks[1], peaks[3]], axis=0), 1)
         peak = jnp.maximum(peak, other[:1])
         backs.append(swap(jnp.maximum(peaks[2], other[1:]), 2))

time: 32.3 us -> 32.1 us (level)
  waiting for transfers between devices: 5.98 us -> 4.06 us
  Pallas kernels: 7.48 us -> 8.47 us
  starting transfers between devices: 12.4 us -> 13.1 us
    ppermute x3, waiting for transfers between devices: 2.13 us -> 0.01 us  [swap(): return lax.ppermute(x, AXES, [(d, d ^ k) for d in range(total)])]
    ppermute x2, starting transfers between devices: 5.37 us -> 7.35 us  [per_device(): visitors = [lax.ppermute(own, AXES, move) for move in moves]]
    ppermute x2, waiting for transfers between devices: 0.75 us -> 2.3 us  [per_device(): backs.append(lax.ppermute(back, AXES, home + list(zip(idle, alone))))]
    ppermute x2, waiting for transfers between devices: 3.1 us -> 1.76 us  [per_device(): visitors = [lax.ppermute(own, AXES, move) for move in moves]]
    ppermute x2, starting transfers between devices: 3.96 us -> 2.66 us  [per_device(): backs.append(lax.ppermute(back, AXES, home + list(zip(idle, alone))))]
    pallas_call x4 -> x5, Pallas kernels: 5.26 us -> 6.25 us  [meet(): pl.pallas_call(functools.partial(meet_kernel, ids, slots, len(held), len(...]
  transfers between devices with their start and end apart: 7 -> 7, of which waited for: 5 -> 4; matrix products, arithmetic and copies ran while one was open for 0% -> 0% of each run, Pallas kernels for 16% -> 20%
where the time goes in v7:
time: 32.1 us; the launch traced here: 31.9 us
  starting transfers between devices  13.1 us (41%)
  Pallas kernels  8.47 us (26%)
  blocking collectives  4.95 us (15%)
  waiting for transfers between devices  4.06 us (13%)
  local copies, waits for them, and re-layouts  0.67 us (2%)
  other arithmetic  0.58 us (2%)
    ppermute x2, starting transfers between devices, per_device(): visitors = [lax.ppermute(own, AXES, move) for move in moves]  7.35 us
    pallas_call x5, Pallas kernels, meet(): pl.pallas_call(functools.partial(meet_kernel, ids, slots, len(held), len(...  6.25 us
    ppermute x3, starting transfers between devices, swap(): return lax.ppermute(x, AXES, [(d, d ^ k) for d in range(total)])  3.04 us
    ppermute x2, starting transfers between devices, per_device(): backs.append(lax.ppermute(back, AXES, home + list(zip(idle, alone))))  2.66 us
    all_gather x1, blocking collectives, per_device(): held = [lax.all_gather(own, 'cols')]  2.58 us
    all_gather x1, blocking collectives, per_device(): held.append(lax.all_gather(across, 'cols'))  2.37 us
    ppermute x2, waiting for transfers between devices, per_device(): backs.append(lax.ppermute(back, AXES, home + list(zip(idle, alone))))  2.3 us
    pallas_call x1, Pallas kernels, per_device(): pl.pallas_call(norm_kernel, out_shape=jax.ShapeDtypeStruct((rows, width),...  2.22 us
  transfers between devices with their start and end apart: 7, of which 4 were waited for; matrix products, arithmetic and copies ran while one was open for 0% of the time, Pallas kernels for 20%

profile of v7, /device:TPU:0, one launch (start us, length us, event | category | flops | bytes accessed | tf_op | source)
XLA Modules:
  0.0 31.9 jit_solution(11786300247055589961)
XLA Ops:
  0.0 2.2 %shard_map.55 = bf16[256,768]{1,0:T(8,128)(2,1)} custom-call(s32[4]{0:T(128)} %size_ref.9, s32[4]{0:T(128)} %start_ref.9, s32[1,256]{1,0:T(1,128)} %bitcast.12, f32[256,768]{1,0:T(8,128)} %emb_hbm.1), custom_call_target="tpu_custom_call" | custom-call | tf_op jit(solution)/shard_map/pallas_call | solution.py:139
  2.2 0.0 copy-start
  2.2 4.1 %collective-permute-start = (bf16[256,768]{1,0:T(8,128)(2,1)}, bf16[256,768]{1,0:T(8,128)(2,1)S(1)}, u32[]{:S(2)}, u32[]{:S(2)}) collective-permute-start(bf16[256,768]{1,0:T(8,128)(2,1)} %shard_map.55), channel_id=1, source_target_pairs={{0,8},{1,9},{2,10},{3,11},{4,0},{5,1},{6,2},{7,3},{8,12},{9,13},{1... | collective-permute-start | bytes 1179656 | tf_op jit(solution)/shard_map/ppermute | solution.py:157
  6.3 1.5 %collective-permute-start.1 = (bf16[256,768]{1,0:T(8,128)(2,1)}, bf16[256,768]{1,0:T(8,128)(2,1)S(1)}, u32[]{:S(2)}, u32[]{:S(2)}) collective-permute-start(bf16[256,768]{1,0:T(8,128)(2,1)} %shard_map.55), channel_id=1, source_target_pairs={{0,2},{1,3},{2,0},{3,1},{4,6},{5,7},{6,4},{7,5},{8,10},{9,11},{10,... | collective-permute-start | bytes 1179656 | tf_op jit(solution)/shard_map/ppermute | solution.py:155
  7.9 3.3 %collective-permute-start.3 = (bf16[256,768]{1,0:T(8,128)(2,1)}, bf16[256,768]{1,0:T(8,128)(2,1)S(1)}, u32[]{:S(2)}, u32[]{:S(2)}) collective-permute-start(bf16[256,768]{1,0:T(8,128)(2,1)} %shard_map.55), channel_id=1, source_target_pairs={{8,4},{9,5},{10,6},{11,7},{0,12},{1,13},{2,14},{3,15},{24,20},{25,... | collective-permute-start | bytes 1179656 | tf_op jit(solution)/shard_map/ppermute | solution.py:157
  11.1 2.6 %all-gather = bf16[512,768]{1,0:T(8,128)(2,1)S(1)} all-gather(bf16[256,768]{1,0:T(8,128)(2,1)} %shard_map.55), channel_id=2, replica_groups=mesh['groups'=2,'rows'=8,'cols'=2] {'cols'}, dimensions={0}, use_global_device_ids=true | all-gather | bytes 1179648 | tf_op jit(solution)/shard_map/all_gather | solution.py:172
  13.7 0.0 copy-start.1
  13.7 0.0 copy-start.2
  13.7 0.0 copy-done
  13.7 0.6 %copy-done.1 = s32[4]{0:T(128)S(1)} copy-done((s32[4]{0:T(128)S(1)}, s32[4]{0:T(128)}, u32[]{:S(2)}) %copy-start.1) | copy-done | bytes 40
  14.4 0.0 copy-done.2
  14.4 1.2 %shard_map.56.refs_2_ = f32[1,256]{1,0:T(1,128)S(1)} custom-call(s32[16,6]{1,0:T(8,128)S(1)} %copy-done, s32[4]{0:T(128)S(1)} %copy-done.1, s32[4]{0:T(128)S(1)} %copy-done.2, bf16[2,256,768]{2,1,0:T(8,128)(2,1)S(1)} %bitcast.4, bf16[2,256,768]{2,1,0:T(8,128)(2,1)S(1)} %bitcast.5), custom_call_target="tpu_custom_call" | custom-call | flops 201326592 | bytes 1179648 | tf_op jit(solution)/shard_map/pallas_call | solution.py:162
  15.6 0.6 %collective-permute-done.refs_0_ = bf16[256,768]{1,0:T(8,128)(2,1)S(1)} collective-permute-done((bf16[256,768]{1,0:T(8,128)(2,1)}, bf16[256,768]{1,0:T(8,128)(2,1)S(1)}, u32[]{:S(2)}, u32[]{:S(2)}) %collective-permute-start) | collective-permute-done | bytes 393248 | tf_op jit(solution)/shard_map/ppermute | solution.py:157
  16.2 1.2 %shard_map.57 = (f32[1,256]{1,0:T(1,128)S(1)}, f32[1,256]{1,0:T(1,128)S(1)}, f32[1,256]{1,0:T(1,128)S(1)}) custom-call(s32[16,6]{1,0:T(8,128)S(1)} %copy-done, s32[4]{0:T(128)S(1)} %copy-done.1, s32[4]{0:T(128)S(1)} %copy-done.2, bf16[256,768]{1,0:T(8,128)(2,1)S(1)} %collective-permute-done.refs_0_, bf16[2,256,768]{2,1,0:T(8,128)(2,1)S(1)} %bitcast.6, ...), custom_call_target="tpu_custom_call" | custom-call | flops 201326592 | bytes 1179648 | tf_op jit(solution)/shard_map/pallas_call | solution.py:162
  17.4 0.0 collective-permute-done.1
  17.4 2.4 %all-gather.1 = bf16[512,768]{1,0:T(8,128)(2,1)S(1)} all-gather(bf16[256,768]{1,0:T(8,128)(2,1)S(1)} %collective-permute-done.1), channel_id=3, replica_groups=mesh['groups'=2,'rows'=8,'cols'=2] {'cols'}, dimensions={0}, use_global_device_ids=true | all-gather | bytes 1179648 | tf_op jit(solution)/shard_map/all_gather | solution.py:177
  19.8 1.2 %shard_map.58 = (f32[1,256]{1,0:T(1,128)S(1)}, f32[1,256]{1,0:T(1,128)S(1)}, f32[1,256]{1,0:T(1,128)S(1)}) custom-call(s32[16,6]{1,0:T(8,128)S(1)} %copy-done, s32[4]{0:T(128)S(1)} %copy-done.1, s32[4]{0:T(128)S(1)} %copy-done.2, bf16[256,768]{1,0:T(8,128)(2,1)S(1)} %collective-permute-done.refs_0_, bf16[2,256,768]{2,1,0:T(8,128)(2,1)S(1)} %bitcast.9, ...), custom_call_target="tpu_custom_call" | custom-call | flops 201326592 | bytes 1179648 | tf_op jit(solution)/shard_map/pallas_call | solution.py:162
  21.0 1.3 %collective-permute-start.2 = (f32[1,256]{1,0:T(1,128)S(1)}, f32[1,256]{1,0:T(1,128)S(1)}, u32[]{:S(2)}, u32[]{:S(2)}) collective-permute-start(f32[1,256]{1,0:T(1,128)S(1)} %get-tuple-element.28), channel_id=1, source_target_pairs={{8,0},{9,1},{10,2},{11,3},{0,4},{1,5},{2,6},{3,7},{12,8},{13,9},{1... | collective-permute-start | bytes 3080 | tf_op jit(solution)/shard_map/ppermute | solution.py:188
  22.3 1.2 %collective-permute-done.3.refs_0_ = bf16[256,768]{1,0:T(8,128)(2,1)S(1)} collective-permute-done((bf16[256,768]{1,0:T(8,128)(2,1)}, bf16[256,768]{1,0:T(8,128)(2,1)S(1)}, u32[]{:S(2)}, u32[]{:S(2)}) %collective-permute-start.3) | collective-permute-done | bytes 393248 | tf_op jit(solution)/shard_map/ppermute | solution.py:157
  23.5 1.4 %shard_map.59 = (f32[1,256]{1,0:T(1,128)S(1)}, f32[1,256]{1,0:T(1,128)S(1)}, f32[1,256]{1,0:T(1,128)S(1)}, f32[1,256]{1,0:T(1,128)S(1)}, f32[1,256]{1,0:T(1,128)S(1)}) custom-call(s32[16,6]{1,0:T(8,128)S(1)} %copy-done, s32[4]{0:T(128)S(1)} %copy-done.1, s32[4]{0:T(128)S(1)} %copy-done.2, bf16[256,768]{1,0:T(8,128)(2,1)S(1)} %collective-permute-done.3.refs_0_, ...), custom_call_target="tpu_custom_call" | custom-call | flops 402653184 | bytes 1966080 | tf_op jit(solution)/shard_map/pallas_call | solution.py:162
  24.9 1.0 %collective-permute-done.2 = f32[1,256]{1,0:T(1,128)S(1)} collective-permute-done((f32[1,256]{1,0:T(1,128)S(1)}, f32[1,256]{1,0:T(1,128)S(1)}, u32[]{:S(2)}, u32[]{:S(2)}) %collective-permute-start.2) | collective-permute-done | bytes 1056 | tf_op jit(solution)/shard_map/ppermute | solution.py:188
  25.9 0.0 collective-permute-start.4
  25.9 1.4 %collective-permute-start.5 = (f32[1,256]{1,0:T(1,128)S(1)}, f32[1,256]{1,0:T(1,128)S(1)}, u32[]{:S(2)}, u32[]{:S(2)}) collective-permute-start(f32[1,256]{1,0:T(1,128)S(1)} %get-tuple-element.41), channel_id=1, source_target_pairs={{4,8},{5,9},{6,10},{7,11},{12,0},{13,1},{14,2},{15,3},{0,4},{1,5},... | collective-permute-start | bytes 3080 | tf_op jit(solution)/shard_map/ppermute | solution.py:188
  27.3 0.0 collective-permute-done.4
  27.3 1.5 %collective-permute-start.6 = (f32[1,256]{1,0:T(1,128)S(1)}, f32[1,256]{1,0:T(1,128)S(1)}, u32[]{:S(2)}, u32[]{:S(2)}) collective-permute-start(f32[1,256]{1,0:T(1,128)S(1)} %slice_maximum_fusion), channel_id=1, source_target_pairs={{0,2},{1,3},{2,0},{3,1},{4,6},{5,7},{6,4},{7,5},{8,10},{9,11},{10,... | collective-permute-start | bytes 3080 | tf_op jit(solution)/shard_map/ppermute | solution.py:155
  28.8 1.2 %shard_map.60 = f32[1,256]{1,0:T(1,128)S(1)} custom-call(s32[16,6]{1,0:T(8,128)S(1)} %copy-done, s32[4]{0:T(128)S(1)} %copy-done.1, s32[4]{0:T(128)S(1)} %copy-done.2, bf16[2,256,768]{2,1,0:T(8,128)(2,1)S(1)} %bitcast.8, bf16[2,256,768]{2,1,0:T(8,128)(2,1)S(1)} %bitcast.11), custom_call_target="tpu_custom_call" | custom-call | flops 201326592 | bytes 1179648 | tf_op jit(solution)/shard_map/pallas_call | solution.py:162
  30.0 1.3 %collective-permute-done.5 = f32[1,256]{1,0:T(1,128)S(1)} collective-permute-done((f32[1,256]{1,0:T(1,128)S(1)}, f32[1,256]{1,0:T(1,128)S(1)}, u32[]{:S(2)}, u32[]{:S(2)}) %collective-permute-start.5) | collective-permute-done | bytes 1056 | tf_op jit(solution)/shard_map/ppermute | solution.py:188
  31.3 0.0 collective-permute-done.6
  31.3 0.6 %compare_select_fusion = f32[1,256]{1,0:T(1,128)} fusion(f32[1,256]{1,0:T(1,128)S(1)} %collective-permute-done.6, f32[1,256]{1,0:T(1,128)S(1)} %collective-permute-done.5, f32[1,256]{1,0:T(1,128)S(1)} %collective-permute-done.2, f32[2,256]{1,0:T(2,128)S(1)} %collective-permute-done.4, f32[1,256]{1,0:T(1,128)S(1)} %get-tuple-element.37, f32[1,256]{1,0:T(1,128)S(1)} %shard_map.60), kind=kLoop, calls=%fused_computation | loop fusion | flops 1792 | bytes 7168 | tf_op jit(solution)/shard_map/jit(_where)/select_n | solution.py:202
  (2 shorter events, 0.0 us)
Async XLA Ops:
  2.2 11.5 %copy-start = (s32[16,6]{1,0:T(8,128)S(1)}, s32[16,6]{1,0:T(8,128)}, u32[]{:S(2)}) copy-start(s32[16,6]{1,0:T(8,128)} %constant.6.clone.table_ref) | copy-start | bytes 1156
  2.2 13.9 %collective-permute-start = (bf16[256,768]{1,0:T(8,128)(2,1)}, bf16[256,768]{1,0:T(8,128)(2,1)S(1)}, u32[]{:S(2)}, u32[]{:S(2)}) collective-permute-start(bf16[256,768]{1,0:T(8,128)(2,1)} %shard_map.55), channel_id=1, source_target_pairs={{0,8},{1,9},{2,10},{3,11},{4,0},{5,1},{6,2},{7,3},{8,12},{9,13},{1... | collective-permute-start | bytes 1179656 | tf_op jit(solution)/shard_map/ppermute | solution.py:157
  6.3 11.1 %collective-permute-start.1 = (bf16[256,768]{1,0:T(8,128)(2,1)}, bf16[256,768]{1,0:T(8,128)(2,1)S(1)}, u32[]{:S(2)}, u32[]{:S(2)}) collective-permute-start(bf16[256,768]{1,0:T(8,128)(2,1)} %shard_map.55), channel_id=1, source_target_pairs={{0,2},{1,3},{2,0},{3,1},{4,6},{5,7},{6,4},{7,5},{8,10},{9,11},{10,... | collective-permute-start | bytes 1179656 | tf_op jit(solution)/shard_map/ppermute | solution.py:155
  7.9 15.6 %collective-permute-start.3 = (bf16[256,768]{1,0:T(8,128)(2,1)}, bf16[256,768]{1,0:T(8,128)(2,1)S(1)}, u32[]{:S(2)}, u32[]{:S(2)}) collective-permute-start(bf16[256,768]{1,0:T(8,128)(2,1)} %shard_map.55), channel_id=1, source_target_pairs={{8,4},{9,5},{10,6},{11,7},{0,12},{1,13},{2,14},{3,15},{24,20},{25,... | collective-permute-start | bytes 1179656 | tf_op jit(solution)/shard_map/ppermute | solution.py:157
  13.7 0.7 %copy-start.1 = (s32[4]{0:T(128)S(1)}, s32[4]{0:T(128)}, u32[]{:S(2)}) copy-start(s32[4]{0:T(128)} %size_ref.9) | copy-start | bytes 52
  13.7 0.7 %copy-start.2 = (s32[4]{0:T(128)S(1)}, s32[4]{0:T(128)}, u32[]{:S(2)}) copy-start(s32[4]{0:T(128)} %start_ref.9) | copy-start | bytes 52
  21.0 4.9 %collective-permute-start.2 = (f32[1,256]{1,0:T(1,128)S(1)}, f32[1,256]{1,0:T(1,128)S(1)}, u32[]{:S(2)}, u32[]{:S(2)}) collective-permute-start(f32[1,256]{1,0:T(1,128)S(1)} %get-tuple-element.28), channel_id=1, source_target_pairs={{8,0},{9,1},{10,2},{11,3},{0,4},{1,5},{2,6},{3,7},{12,8},{13,9},{1... | collective-permute-start | bytes 3080 | tf_op jit(solution)/shard_map/ppermute | solution.py:188
  25.9 1.4 %collective-permute-start.4 = (f32[2,256]{1,0:T(2,128)S(1)}, f32[2,256]{1,0:T(2,128)S(1)}, u32[]{:S(2)}, u32[]{:S(2)}) collective-permute-start(f32[2,256]{1,0:T(2,128)S(1)} %pad_maximum_fusion), channel_id=1, source_target_pairs={{0,1},{1,0},{2,3},{3,2},{4,5},{5,4},{6,7},{7,6},{8,9},{9,8},{10,11... | collective-permute-start | bytes 6152 | tf_op jit(solution)/shard_map/ppermute | solution.py:155
  25.9 5.4 %collective-permute-start.5 = (f32[1,256]{1,0:T(1,128)S(1)}, f32[1,256]{1,0:T(1,128)S(1)}, u32[]{:S(2)}, u32[]{:S(2)}) collective-permute-start(f32[1,256]{1,0:T(1,128)S(1)} %get-tuple-element.41), channel_id=1, source_target_pairs={{4,8},{5,9},{6,10},{7,11},{12,0},{13,1},{14,2},{15,3},{0,4},{1,5},... | collective-permute-start | bytes 3080 | tf_op jit(solution)/shard_map/ppermute | solution.py:188
  27.3 4.0 %collective-permute-start.6 = (f32[1,256]{1,0:T(1,128)S(1)}, f32[1,256]{1,0:T(1,128)S(1)}, u32[]{:S(2)}, u32[]{:S(2)}) collective-permute-start(f32[1,256]{1,0:T(1,128)S(1)} %slice_maximum_fusion), channel_id=1, source_target_pairs={{0,2},{1,3},{2,0},{3,1},{4,6},{5,7},{6,4},{7,5},{8,10},{9,11},{10,... | collective-permute-start | bytes 3080 | tf_op jit(solution)/shard_map/ppermute | solution.py:155
